TPU v7x, 32 devices: a whole 2x2x4 slice. The times are simulated.
32 devices in a mesh: wide: 16 (over z, y, core), narrow: 2 (over x).
Axes of the slice: x: 2, y: 2, z: 4, core: 2. Of those that a mesh axis runs over, the one named last changes fastest.
Arguments:
- tokens: bfloat16 [384, 128, 512], P(('wide', 'narrow')), may hold values from -6 to 6
- memory: bfloat16 [384, 256, 512], P(('wide', 'narrow')), may hold values from -6 to 6
- cotangent: bfloat16 [384, 128, 512], P(('wide', 'narrow')), may hold values from -6 to 6
- dec_segments: int32 [384, 128], P(('wide', 'narrow')), may hold values from 0 to 3, never falling along the last dimension, each value on 1 to 64 neighbouring positions
- mem_segments: int32 [384, 256], P(('wide', 'narrow')), may hold values from 0 to 3, never falling along the last dimension, each value on 1 to 128 neighbouring positions
- padding: int32 [384, 128], P(('wide', 'narrow')), may hold values 0 or 1
- buckets: int32 [128], replicated, may hold values from 0 to 31, as said below
- w_query: bfloat16 [512, 512], P(('wide', 'narrow')), may hold values from -0.03125 to 0.03125
- w_key: bfloat16 [512, 512], P(('wide', 'narrow')), may hold values from -0.25 to 0.25
- w_value: bfloat16 [512, 512], P(('wide', 'narrow')), may hold values from -0.25 to 0.25
- w_out: bfloat16 [512, 512], P(('wide', 'narrow')), may hold values from -1 to 1
- c_query: bfloat16 [512, 512], P(('wide', 'narrow')), may hold values from -0.03125 to 0.03125
- c_key: bfloat16 [512, 512], P(('wide', 'narrow')), may hold values from -0.25 to 0.25
- c_value: bfloat16 [512, 512], P(('wide', 'narrow')), may hold values from -0.25 to 0.25
- c_out: bfloat16 [512, 512], P(('wide', 'narrow')), may hold values from -1.5 to 1.5
- w_hidden: bfloat16 [512, 2048], P(('wide', 'narrow')), may hold values from -0.25 to 0.25
- w_back: bfloat16 [2048, 512], P(('wide', 'narrow')), may hold values from -0.1875 to 0.1875
- gain_self: bfloat16 [512], P(('wide', 'narrow')), may hold values from 0.2 to 4
- gain_cross: bfloat16 [512], P(('wide', 'narrow')), may hold values from 0.2 to 4
- gain_ff: bfloat16 [512], P(('wide', 'narrow')), may hold values from 0.2 to 4
- bias_table: bfloat16 [256], P(('wide', 'narrow')), may hold values from -4 to 4
Outputs:
- result: bfloat16 [384, 128, 512], P(('wide', 'narrow'))
- grad_tokens: bfloat16 [384, 128, 512], P(('wide', 'narrow'))
- grad_memory: bfloat16 [384, 256, 512], P(('wide', 'narrow'))
- grad_w_query: float32 [512, 512], P(('wide', 'narrow'))
- grad_w_key: float32 [512, 512], P(('wide', 'narrow'))
- grad_w_value: float32 [512, 512], P(('wide', 'narrow'))
- grad_w_out: float32 [512, 512], P(('wide', 'narrow'))
- grad_c_query: float32 [512, 512], P(('wide', 'narrow'))
- grad_c_key: float32 [512, 512], P(('wide', 'narrow'))
- grad_c_value: float32 [512, 512], P(('wide', 'narrow'))
- grad_c_out: float32 [512, 512], P(('wide', 'narrow'))
- grad_w_hidden: float32 [512, 2048], P(('wide', 'narrow'))
- grad_w_back: float32 [2048, 512], P(('wide', 'narrow'))
- grad_gain_self: float32 [512], P(('wide', 'narrow'))
- grad_gain_cross: float32 [512], P(('wide', 'narrow'))
- grad_gain_ff: float32 [512], P(('wide', 'narrow'))
- grad_bias_table: float32 [256], P(('wide', 'narrow'))
- example_norms: float32 [384, 4], P(('wide', 'narrow'))
- global_norm: float32 [], replicated
Inputs may be any that keep to these rules, and one draw needn't show every extreme that they name: buckets never falls as the distance grows; buckets[0] = 0 and buckets[127] = 31. `dec_segments`: along a row the example numbers never fall; each of the 4 examples has 1 to 64 decoder tokens. `mem_segments`: along a row the example numbers never fall; each of the 4 examples has 1 to 128 memory tokens.
All inputs are finite; a program needn't handle non-finite values. No bound on the sum of `padding` on one device may be relied on, other than what follows from the above.
Results may differ from a plain program's by a relative error of at most 0.014.
Values may be sent and summed in bfloat16 or wider, within the bound.
No kernel may reach another device: no remote copies, remote signals or barrier semaphores. Data moves between devices by JAX's collectives and lax.ppermute only.
A program may use at most 192 MiB of HBM per device.

v0:
```python
import math
from functools import partial

import jax
import jax.numpy as jnp
from jax import lax
from jax.experimental import pallas as pl
from jax.experimental.pallas import tpu as pltpu
from jax.sharding import PartitionSpec as P

H = 8
DH = 64
NB = 32
NSEG = 4
COUNT = 4196096
EPSILON = 1e-06
FLOOR = -1e30
F32 = jnp.float32
BF16 = jnp.bfloat16
PAIRS = H // 2
LANES = 128
STEP_ROWS = 4
SMALL_ROWS = 4
VMEM_LIMIT = 60 * 2**20
SHARED_LIMIT = 48 * 2**20

COLUMN = (0, 8, 16, 24)
PLANE = (0, 1, 4, 5)
CODES = tuple(2 * c + mask + z for c in (0, 1) for mask in PLANE for z in COLUMN)


def nn(left, right):
    return lax.dot_general(left, right, (((1,), (0,)), ((), ())), preferred_element_type=F32)


def nt(left, right):
    return lax.dot_general(left, right, (((1,), (1,)), ((), ())), preferred_element_type=F32)


def tn(left, right):
    return lax.dot_general(left, right, (((0,), (0,)), ((), ())), preferred_element_type=F32)


def inverse_root(values):
    return lax.rsqrt(jnp.mean(values * values, axis=-1, keepdims=True) + EPSILON)


def head_masks(values):
    low = (lax.broadcasted_iota(jnp.int32, (1, LANES), 1) < DH).astype(BF16)
    return values * low, values * (1 - low)


def head_pair(values):
    return jnp.concatenate(head_masks(values), axis=0)


def fold_pair(both, queries):
    own = jnp.concatenate([both[:DH, :queries], both[DH:, queries:]], axis=0)
    return own.astype(BF16).T


def block_rows(block):
    return pl.ds(pl.multiple_of(block * 16, 16), 16)


def start_copies(pairs, sems):
    copies = [pltpu.make_async_copy(*pair, sems.at[i]) for i, pair in enumerate(pairs)]
    for copy in copies:
        copy.start()
    return copies


def read_rows(grad_w, block):
    return grad_w[block_rows(block), :].astype(BF16)


def store_slots(me_ref, low_ref, high_ref, read):
    for k, code in enumerate(CODES):
        target = low_ref if k < 16 else high_ref
        target[k % 16] = read(me_ref[0] ^ code)


def softmax_columns(scores):
    shifted = jnp.exp(scores - jnp.max(scores, axis=0, keepdims=True))
    return (shifted * (1.0 / jnp.sum(shifted, axis=0, keepdims=True))).astype(BF16)


def step_rows(ref, step, count):
    whole = ref[...].astype(F32)
    rows = whole[:count]
    for s in range(1, whole.shape[0] // count):
        rows = jnp.where(step == s, whole[s * count : (s + 1) * count], rows)
    return rows


def token_columns(lines):
    pad = 8 - lines.shape[0] % 8
    return jnp.concatenate([lines] + [lines[:1]] * (pad % 8), axis=0).T


def member_lines(lines):
    count, length = lines.shape
    codes = jnp.concatenate([lines[r : r + 1] + float(NSEG * r) for r in range(count)], axis=1)
    places = lax.broadcasted_iota(jnp.int32, (NSEG * count, count * length), 0).astype(F32)
    return (codes == places).astype(F32).astype(BF16)


def same_sum(products, lines, columns, r):
    same = columns[:, r : r + 1] == lines[r : r + 1]
    return jnp.sum(jnp.where(same, products, 0.0), axis=0, keepdims=True)


def pipelined(items, *stages):
    state = {}
    for tick in range(len(items) + len(stages) - 1):
        for depth, stage in enumerate(stages):
            n = tick - depth
            if 0 <= n < len(items):
                state[n] = stage(items[n], state.get(n))


def row_pairs(count):
    return [(r, p) for r in range(count) for p in range(PAIRS)]


def gram(left):
    return nt(left, left)


def self_forward_kernel(me_ref, tokens_ref, dec_ref, padding_ref, buckets_ref, *refs):
    pieces, refs = refs[:8], refs[8:]
    input_ref, qkv_ref, prob_ref, attended_ref, weight_ref, gains_ref = refs[:6]
    bias_ref, small_ref, sems = refs[6:]
    length = dec_ref.shape[1]
    width = tokens_ref.shape[1]

    @pl.when(pl.program_id(0) == 0)
    def _():
        pairs = []
        for k, code in enumerate(CODES):
            rows = block_rows(me_ref[0] ^ code)
            source = pieces[k // 4].at[k % 4]
            pairs.append((source.at[:, : 3 * width], weight_ref.at[rows, :]))
            pairs.append((source.at[:, 3 * width :], small_ref.at[rows, :]))
        for copy in start_copies(pairs, sems):
            copy.wait()
        first = lax.broadcasted_iota(jnp.int32, (32, width), 1)
        pick = first == 16 * lax.broadcasted_iota(jnp.int32, (32, width), 0)
        small = nn(pick.astype(F32).astype(BF16), small_ref[...]).astype(BF16)
        lane = lax.broadcasted_iota(jnp.int32, (LANES, width), 0)
        feature = lax.broadcasted_iota(jnp.int32, (LANES, width), 1)
        block = lax.broadcasted_iota(jnp.int32, (32, width), 0)
        lines = []
        for k in range(4):
            spread = nn(small, (lane == 16 * k + feature % 16).astype(F32).astype(BF16))
            lines.append(
                jnp.sum(jnp.where(block == first // 16, spread, 0.0), axis=0, keepdims=True)
            )
        gains_ref[...] = jnp.concatenate(lines + lines, axis=0)
        place = lax.broadcasted_iota(jnp.int32, (H, width), 1) % 16
        head = lax.broadcasted_iota(jnp.int32, (H, width), 0)
        table = jnp.where(place == head, lines[3], 0.0).astype(BF16)
        bucket = lax.broadcasted_iota(jnp.int32, (width, length), 0) // 16
        curves = nn(table, (bucket == buckets_ref[...]).astype(F32).astype(BF16))
        for h in range(H):
            curve = jnp.broadcast_to(curves[h : h + 1, :], (length, length))
            lanes = slice((h % 2) * length, (h % 2 + 1) * length)
            bias_ref[h // 2, :, lanes] = pltpu.roll(curve, 0, 1, stride=1, stride_axis=0)

    values = tokens_ref[...].astype(F32)
    normed = (values * inverse_root(values) * gains_ref[0:1, :]).astype(BF16)
    input_ref[...] = normed
    for first in range(0, 3 * width, 256):
        cols = slice(first, first + 256)
        qkv_ref[:, cols] = nn(normed, weight_ref[:, cols]).astype(BF16)

    step = pl.program_id(0)
    count = tokens_ref.shape[0] // length
    segments, real = step_rows(dec_ref, step, count), step_rows(padding_ref, step, count)
    segment_columns, real_columns = token_columns(segments), token_columns(real)
    key_i = lax.broadcasted_iota(jnp.int32, (length, length), 0)
    query_i = lax.broadcasted_iota(jnp.int32, (length, length), 1)

    masks = []
    for r in range(count):
        allowed = (segment_columns[:, r : r + 1] == segments[r : r + 1]) & (key_i <= query_i)
        allowed = allowed & ((real_columns[:, r : r + 1] > 0.0) | (key_i == query_i))
        mask = jnp.where(allowed, 0.0, FLOOR)
        masks.append(jnp.concatenate([mask, mask], axis=1))

    def part(item, k):
        r, p = item
        return qkv_ref[r * length : (r + 1) * length, k * width + p * LANES : k * width + (p + 1) * LANES]

    def scores(item, _):
        return nt(part(item, 1), head_pair(part(item, 0)))

    def weigh(item, score):
        r, p = item
        prob = softmax_columns(score + bias_ref[p] + masks[r])
        prob_ref[r, p] = prob
        return prob, part(item, 2).T

    def mix(item, given):
        r, p = item
        prob, value = given
        rows, lanes = slice(r * length, (r + 1) * length), slice(p * LANES, (p + 1) * LANES)
        attended_ref[rows, lanes] = fold_pair(nn(value, prob), length)

    pipelined(row_pairs(count), scores, weigh, mix)


def memory_forward_kernel(me_ref, memory_ref, *refs):
    pieces, (kv_ref, weight_ref, sems) = refs[:-3], refs[-3:]
    width = memory_ref.shape[1]

    @pl.when(pl.program_id(0) == 0)
    def _():
        pairs = []
        for k, code in enumerate(CODES):
            source = pieces[k // 4].at[k % 4]
            pairs.append((source, weight_ref.at[block_rows(me_ref[0] ^ code), :]))
        for copy in start_copies(pairs, sems):
            copy.wait()

    for first in range(0, 2 * width, 256):
        kv_ref[:, first : first + 256] = nn(
            memory_ref[...], weight_ref[:, 2 * width + first : 2 * width + first + 256]
        ).astype(BF16)


def cross_forward_kernel(tokens_ref, attended_a_ref, kv_ref, dec_ref, mem_ref, gains_ref,
                         weight_ref, middle_ref, input_ref, query_ref, prob_ref, attended_ref, after_ref):
    mem_length, length = mem_ref.shape[1], dec_ref.shape[1]
    width = tokens_ref.shape[1]
    values = tokens_ref[...].astype(F32) + nn(attended_a_ref[...], weight_ref[:, :width])
    middle_ref[...] = values.astype(BF16)
    normed = (values * inverse_root(values) * gains_ref[1:2, :]).astype(BF16)
    input_ref[...] = normed
    query_ref[...] = nn(normed, weight_ref[:, width : 2 * width]).astype(BF16)

    step = pl.program_id(0)
    count = tokens_ref.shape[0] // length
    segments = step_rows(dec_ref, step, count)
    mem_columns = token_columns(step_rows(mem_ref, step, count))

    masks = []
    for r in range(count):
        mask = jnp.where(mem_columns[:, r : r + 1] == segments[r : r + 1], 0.0, FLOOR)
        masks.append(jnp.concatenate([mask, mask], axis=1))

    def places(item):
        r, p = item
        rows, lanes = slice(r * length, (r + 1) * length), slice(p * LANES, (p + 1) * LANES)
        upper = slice(width + p * LANES, width + (p + 1) * LANES)
        return rows, slice(r * mem_length, (r + 1) * mem_length), lanes, upper

    def scores(item, _):
        rows, mem_rows, lanes, _ = places(item)
        return nt(kv_ref[mem_rows, lanes], head_pair(query_ref[rows, lanes]))

    def weigh(item, score):
        r, p = item
        _, mem_rows, _, upper = places(item)
        prob = softmax_columns(score + masks[r])
        prob_ref[r, p] = prob
        return prob, kv_ref[mem_rows, upper].T

    def mix(item, given):
        rows, _, lanes, _ = places(item)
        prob, value = given
        attended_ref[rows, lanes] = fold_pair(nn(value, prob), length)

    pipelined(row_pairs(count), scores, weigh, mix)
    after = values + nn(attended_ref[...], weight_ref[:, 4 * width :])
    after_ref[...] = after.astype(BF16)


def norm_back(values, gain, grad_normed):
    inverse = inverse_root(values)
    scaled = values * inverse
    upper = grad_normed * gain
    grad = inverse * (upper - scaled * jnp.mean(upper * scaled, axis=-1, keepdims=True))
    return grad, grad_normed * scaled


def gain_sums(terms, segments, total_ref, square_ref):
    sums = nn(member_lines(segments), terms.astype(BF16))
    total_ref[...] += jnp.sum(sums, axis=0, keepdims=True)
    square = jnp.sum(sums * sums, axis=1, keepdims=True)
    square_ref[...] = jnp.broadcast_to(square, square_ref.shape)


def feed_kernel(after_ref, cotangent_ref, dec_ref, padding_ref, gains_ref, gathered_ref,
                result_ref, branch_b_ref, slots_ref, total_ref, square_ref, token_ref, w_in_ref,
                w_out_ref, normed_ref, branch_ref, normed_flip, branch_flip, active_ref, grad_ref,
                in_slots, out_slots, load_sems, sems):
    part = pl.program_id(0)
    parts = pl.num_programs(0)
    count, length = dec_ref.shape
    dec, width = after_ref.shape
    ff = w_in_ref.shape[2]
    tile = STEP_ROWS * length
    tiles = [slice(t * tile, (t + 1) * tile) for t in range(dec // tile)]

    def loads(which):
        rows = pl.ds(pl.multiple_of(which * 16, 16), 16)
        cols = pl.ds(pl.multiple_of(which * width, width), width)
        blocks = pl.ds(which * 8, 8)
        pairs = (
            (gathered_ref.at[:, rows, :], w_in_ref.at[:, :, cols]),
            (gathered_ref.at[blocks, 64:, :], w_out_ref.at[blocks]),
        )
        return [
            pltpu.make_async_copy(*pair, load_sems.at[which, i]) for i, pair in enumerate(pairs)
        ]

    @pl.when(part == 0)
    def _():
        for which in range(ff // width):
            for copy in loads(which):
                copy.start()
        real = token_columns(padding_ref[...].astype(F32))
        for r in range(count):
            rows = slice(r * length, (r + 1) * length)
            branch_ref[rows, :] = (
                cotangent_ref[rows, :].astype(F32) * real[:, r : r + 1]
            ).astype(BF16)
        for rows in tiles:
            values = after_ref[rows, :].astype(F32)
            normed = (values * inverse_root(values) * gains_ref[2:3, :]).astype(BF16)
            normed_ref[rows, :] = normed
            normed_flip[:, rows] = normed.T
            branch_flip[:, rows] = branch_ref[rows, :].T

    for copy in loads(part):
        copy.wait()
    root = 0.7978845608028654
    half_width = width // 2
    for sub in range(2):
        first = pl.multiple_of(part * width + sub * half_width, half_width)
        cols = pl.ds(first, half_width)
        hidden = nn(normed_ref[...], w_in_ref[:, :, cols].reshape(width, half_width))
        square = hidden * hidden
        bent = jnp.tanh(hidden * (root + (root * 0.044715) * square))
        half = 0.5 + 0.5 * bent
        slope = hidden * (2.0 * root + (6.0 * root * 0.044715) * square)
        slope = half + half * (slope * (1.0 - half))
        active_ref[:, cols] = (hidden * half).astype(BF16)
        w_out = w_out_ref[pl.ds(part * 8 + sub * 4, 4)].reshape(half_width, width)
        grad_ref[:, cols] = (nt(branch_ref[...], w_out) * slope).astype(BF16)
    cols = pl.ds(pl.multiple_of(part * width, width), width)
    grad_in = nn(normed_flip[...], grad_ref[:, cols]).astype(BF16)
    grad_out = nn(branch_flip[...], active_ref[:, cols]).astype(BF16).T

    def sends(which):
        pairs = [(in_slots, slots_ref.at[:, pl.ds(pl.multiple_of(which * 16, 16), 16), :])]
        for i, k in enumerate(range(0, 32, 4)):
            pairs.append((out_slots.at[i], slots_ref.at[k + which, 64:, :]))
        return [pltpu.make_async_copy(*pair, sems.at[i]) for i, pair in enumerate(pairs)]

    @pl.when(part > 0)
    def _():
        for copy in sends(part - 1):
            copy.wait()

    for k, block in enumerate(CODES):
        in_slots[k] = grad_in[16 * block : 16 * block + 16]
    for i, k in enumerate(range(0, 32, 4)):
        block = CODES[k]
        out_slots[i] = grad_out[64 * block : 64 * block + 64]
    for copy in sends(part):
        copy.start()

    @pl.when(part == parts - 1)
    def _():
        segments = dec_ref[...].astype(F32)
        columns = token_columns(segments)
        total_ref[...] = jnp.zeros_like(total_ref)
        w_in, w_out = w_in_ref[...].reshape(width, ff), w_out_ref[...].reshape(ff, width)
        for t, rows in enumerate(tiles):
            values = after_ref[rows, :].astype(F32)
            result_ref[rows, :] = (values + nn(active_ref[rows, :], w_out)).astype(BF16)
            grad, terms = norm_back(values, gains_ref[2:3, :], nt(grad_ref[rows, :], w_in))
            branch_b_ref[rows, :] = (branch_ref[rows, :].astype(F32) + grad).astype(BF16)
            own = segments[t * STEP_ROWS : (t + 1) * STEP_ROWS]
            gain_sums(terms, own, total_ref, square_ref.at[t])
        for r in range(count):
            own = slice(r * length, (r + 1) * length)
            products = gram(active_ref[own, :]) * gram(branch_ref[own, :])
            products = products + gram(grad_ref[own, :]) * gram(normed_ref[own, :])
            token_ref[r // STEP_ROWS, r % STEP_ROWS : r % STEP_ROWS + 1, :] = same_sum(
                products, segments, columns, r
            )
        for copy in sends(part):
            copy.wait()


def score_grads(prob, grad_prob):
    prob = prob.astype(F32)
    dots = jnp.sum(prob * grad_prob, axis=0, keepdims=True)
    return prob * (grad_prob - dots)


def cross_backward_kernel(me_ref, branch_ref, middle_ref, memory_ref, attended_a_ref, input_ref,
                          query_ref, kv_ref, prob_ref, attended_ref, dec_ref, gains_ref,
                          weight_ref, grad_query_ref, grad_kv_ref, branch_a_ref, low_ref, high_ref,
                          total_ref, square_ref, grad_w, grad_attended):
    step = pl.program_id(0)
    mem_length = prob_ref.shape[2]
    length = prob_ref.shape[3] // 2
    width = branch_ref.shape[1]

    @pl.when(step == 0)
    def _():
        grad_w[...] = jnp.zeros_like(grad_w)
        total_ref[...] = jnp.zeros_like(total_ref)

    branch = branch_ref[...]
    grad_attended[...] = nt(branch, weight_ref[:, 4 * width :]).astype(BF16)

    def places(item):
        r, p = item
        rows, lanes = slice(r * length, (r + 1) * length), slice(p * LANES, (p + 1) * LANES)
        upper = slice(width + p * LANES, width + (p + 1) * LANES)
        return rows, slice(r * mem_length, (r + 1) * mem_length), lanes, upper

    def enter(item, _):
        rows, mem_rows, lanes, upper = places(item)
        grad_out = head_pair(grad_attended[rows, lanes])
        return grad_out, nt(kv_ref[mem_rows, upper], grad_out)

    def bend(item, given):
        r, p = item
        grad_out, grad_prob = given
        _, mem_rows, lanes, _ = places(item)
        grad_score = score_grads(prob_ref[r, p], grad_prob).astype(BF16)
        return grad_out, grad_score, kv_ref[mem_rows, lanes].T

    def leave(item, given):
        r, p = item
        grad_out, grad_score, key = given
        rows, mem_rows, lanes, upper = places(item)
        query = head_pair(query_ref[rows, lanes])
        grad_kv_ref[mem_rows, lanes] = nn(grad_score, query).astype(BF16)
        grad_kv_ref[mem_rows, upper] = nn(prob_ref[r, p], grad_out).astype(BF16)
        grad_query_ref[rows, lanes] = fold_pair(nn(key, grad_score), length)

    pipelined(row_pairs(STEP_ROWS), enter, bend, leave)
    grad_query = grad_query_ref[...]
    grad_normed = nt(grad_query, weight_ref[:, width : 2 * width])
    grad, terms = norm_back(middle_ref[...].astype(F32), gains_ref[1:2, :], grad_normed)
    branch_a = (branch.astype(F32) + grad).astype(BF16)
    branch_a_ref[...] = branch_a
    gain_sums(terms, step_rows(dec_ref, step, STEP_ROWS), total_ref, square_ref.at[0])
    grad_w[:, :width] += tn(attended_a_ref[...], branch_a)
    grad_w[:, width : 2 * width] += tn(input_ref[...], grad_query)
    grad_w[:, 2 * width : 4 * width] += tn(memory_ref[...], grad_kv_ref[...])
    grad_w[:, 4 * width :] += tn(attended_ref[...], branch)

    @pl.when(step == pl.num_programs(0) - 1)
    def _():
        store_slots(me_ref, low_ref, high_ref, partial(read_rows, grad_w))


def self_scores_kernel(branch_ref, qkv_ref, prob_ref, dec_ref, buckets_ref, weight_ref,
                       grad_qkv_ref, table_ref, table_square_ref, grad_attended, bands):
    step = pl.program_id(0)
    length = prob_ref.shape[2]
    width = branch_ref.shape[1]
    grad_attended[...] = nt(branch_ref[...], weight_ref[:, :width]).astype(BF16)

    @pl.when(step == 0)
    def _():
        table_ref[...] = jnp.zeros_like(table_ref)
        bands[...] = jnp.zeros_like(bands)

    row_i = lax.broadcasted_iota(jnp.int32, (length, length), 0)
    col_i = lax.broadcasted_iota(jnp.int32, (length, length), 1)
    flip = (row_i + col_i == length - 1).astype(F32).astype(BF16)
    columns = token_columns(step_rows(dec_ref, step, STEP_ROWS)).astype(BF16)
    turned = nn(flip, columns)

    members = [
        [
            jnp.broadcast_to((turned[:, r : r + 1] == float(e)).astype(F32), (length, length))
            for e in range(NSEG)
        ]
        for r in range(STEP_ROWS)
    ]

    def part(item, k):
        r, p = item
        lanes = slice(k * width + p * LANES, k * width + (p + 1) * LANES)
        return slice(r * length, (r + 1) * length), lanes

    def enter(item, _):
        grad_out = head_pair(grad_attended[part(item, 0)])
        return grad_out, nt(qkv_ref[part(item, 2)], grad_out)

    def bend(item, given):
        r, p = item
        grad_out, grad_prob = given
        grad_score = score_grads(prob_ref[r, p], grad_prob).astype(BF16)
        return grad_out, grad_score, jnp.concatenate([qkv_ref[part(item, 1)].T, flip], axis=0)

    def leave(item, given):
        r, p = item
        grad_out, grad_score, key = given
        query = head_pair(qkv_ref[part(item, 0)])
        grad_qkv_ref[part(item, 1)] = nn(grad_score, query).astype(BF16)
        grad_qkv_ref[part(item, 2)] = nn(prob_ref[r, p], grad_out).astype(BF16)
        both = nn(key, grad_score)
        grad_qkv_ref[part(item, 0)] = fold_pair(both[:length], length)
        return both[length:]

    def count_buckets(item, turned_score):
        r, p = item
        for h in range(2):
            own = turned_score[:, h * length : (h + 1) * length]
            own = pltpu.roll(own, 1, 1, stride=1, stride_axis=0)
            for e in range(NSEG):
                bands[r, 2 * p + h, e : e + 1, :] = jnp.sum(
                    own * members[r][e], axis=0, keepdims=True
                )

    pipelined(row_pairs(STEP_ROWS), enter, bend, leave, count_buckets)
    bucket = lax.broadcasted_iota(jnp.int32, (LANES, length), 0)
    near = (bucket == buckets_ref[...]).astype(F32)
    flat = bands[...].reshape(STEP_ROWS * H * 8, length)
    per_bucket = lax.dot_general(
        flat, near, (((1,), (1,)), ((), ())), preferred_element_type=F32,
        precision=lax.Precision.HIGHEST,
    ).reshape(STEP_ROWS, H, 8, LANES)
    table_ref[...] += jnp.sum(jnp.sum(per_bucket, axis=0), axis=1)
    squares = jnp.sum(jnp.sum(per_bucket * per_bucket, axis=1), axis=-1, keepdims=True)
    table_square_ref[0] = jnp.broadcast_to(squares, (STEP_ROWS, 8, LANES))


def self_weights_kernel(me_ref, branch_ref, tokens_ref, input_ref, grad_qkv_ref, dec_ref,
                        gains_ref, weight_ref, table_ref, total_b_ref, total_c_ref,
                        grad_tokens_ref, low_ref, high_ref, square_ref, grad_w, total_ref,
                        small_ref):
    step = pl.program_id(0)
    width = tokens_ref.shape[1]
    grad_qkv = grad_qkv_ref[...]
    grad_normed = nt(grad_qkv, weight_ref[...])
    grad, terms = norm_back(tokens_ref[...].astype(F32), gains_ref[0:1, :], grad_normed)
    grad_tokens_ref[...] = (branch_ref[...].astype(F32) + grad).astype(BF16)

    @pl.when(step == 0)
    def _():
        grad_w[...] = jnp.zeros_like(grad_w)
        total_ref[...] = jnp.zeros_like(total_ref)

    gain_sums(terms, step_rows(dec_ref, step, STEP_ROWS), total_ref, square_ref.at[0])
    flipped = input_ref[...].T
    for first in range(0, 3 * width, 256):
        grad_w[:, first : first + 256] += nn(flipped, grad_qkv_ref[:, first : first + 256])

    @pl.when(step == pl.num_programs(0) - 1)
    def _():
        bucket = lax.broadcasted_iota(jnp.int32, (LANES, width), 0)
        place = lax.broadcasted_iota(jnp.int32, (LANES, width), 1)
        spread = nn(table_ref[...].astype(BF16), (place // 16 == bucket).astype(F32).astype(BF16))
        head = lax.broadcasted_iota(jnp.int32, (H, width), 0)
        lane = lax.broadcasted_iota(jnp.int32, (H, width), 1)
        table = jnp.sum(jnp.where(lane % 16 == head, spread, 0.0), axis=0, keepdims=True)
        small = jnp.zeros((LANES, width), F32)
        row_i = lax.broadcasted_iota(jnp.int32, (LANES, width), 0)
        for k, line in enumerate((total_ref[...], total_b_ref[...], total_c_ref[...], table)):
            small = jnp.where(row_i == k, line, small)
        small_ref[...] = small.T

        def read(block):
            return jnp.concatenate(
                [read_rows(grad_w, block), read_rows(small_ref, block)], axis=1
            )

        store_slots(me_ref, low_ref, high_ref, read)


def pair_sum_kernel(low_ref, sent_ref, *refs):
    outs, (low, sent, total, load_sems, store_sems) = refs[:4], refs[4:]
    places = [pl.ds(4 * t, 4) for t in range(4)]
    lows = start_copies([(low_ref.at[p], low.at[p]) for p in places], load_sems.at[0])
    sents = start_copies([(sent_ref.at[p], sent.at[p]) for p in places], load_sems.at[1])
    stores = []
    for t, p in enumerate(places):
        lows[t].wait()
        sents[t].wait()
        total[p] = (low[p].astype(F32) + sent[p].astype(F32)).astype(BF16)
        stores.append(pltpu.make_async_copy(total.at[p], outs[t], store_sems.at[t]))
        stores[t].start()
    for store in stores:
        store.wait()


def pair_sum(low, sent, after):
    piece = shape_of((4,) + low.shape[1:], BF16)
    return pl.pallas_call(
        ignoring(pair_sum_kernel, 2, len(after)),
        out_shape=(piece,) * 4,
        in_specs=[pl.BlockSpec(memory_space=pl.ANY)] * (2 + len(after)),
        out_specs=[pl.BlockSpec(memory_space=pl.ANY)] * 4,
        scratch_shapes=[pltpu.VMEM(low.shape, BF16)] * 3
        + [pltpu.SemaphoreType.DMA((2, 4)), pltpu.SemaphoreType.DMA((4,))],
        compiler_params=pltpu.CompilerParams(vmem_limit_bytes=SHARED_LIMIT),
    )(in_hbm(low), sent, *after)


def plane_sum_kernel(*refs):
    own_ref, outs = refs[8], refs[9:]
    start = 0
    for group in (refs[:4], refs[4:8]):
        cols = slice(start, start + group[0].shape[2])
        start = cols.stop
        for s in range(4):
            total = sum(ref[s].astype(F32) for ref in group)
            if s == 0:
                own_ref[:, cols] = total
            else:
                outs[s - 1][:, cols] = total.astype(BF16)


def plane_sum(groups, after):
    line = (16, sum(group[0].shape[2] for group in groups))
    return small_call(
        plane_sum_kernel, [*groups[0], *groups[1]], after,
        (shape_of(line, F32),) + (shape_of(line, BF16),) * 3,
    )


def square_sum(values):
    return jnp.sum(jnp.sum(values * values, axis=0, keepdims=True), axis=1, keepdims=True)


def feed_end_kernel(sum_ref, hidden_ref, back_ref, square_ref):
    total = sum_ref[...].astype(F32)
    width = total.shape[1]
    for j in range(4):
        hidden_ref[:, j * width : (j + 1) * width] = total[16 * j : 16 * (j + 1)]
    back_ref[...] = total[64:]
    square_ref[...] = jnp.broadcast_to(square_sum(total), square_ref.shape)


def column_end_kernel(own_ref, b_ref, c_ref, d_ref, *refs):
    squares, outs, square_ref = refs[:1], refs[1:-1], refs[-1]
    total = own_ref[...] + b_ref[...].astype(F32)
    total = total + c_ref[...].astype(F32) + d_ref[...].astype(F32)
    start = 0
    for out in outs:
        out[...] = total[:, start : start + out.shape[1]]
        start += out.shape[1]
    square = square_sum(total)
    for given in squares:
        square = square + given[0:1, 0:1]
    square_ref[...] = jnp.broadcast_to(square, square_ref.shape)


def staged(kernel, ins, outs):
    def run(*refs):
        count = ins + outs
        given, inner, sems = refs[:count], refs[count : 2 * count], refs[2 * count]
        for copy in start_copies(list(zip(given[:ins], inner[:ins])), sems):
            copy.wait()
        kernel(*inner)
        for copy in start_copies(list(zip(inner[ins:], given[ins:])), sems):
            copy.wait()

    return run


def small_call(kernel, ins, after, outs):
    arrays = [*ins, *outs]
    return pl.pallas_call(
        ignoring(staged(kernel, len(ins), len(outs)), len(ins), len(after)),
        out_shape=outs,
        in_specs=[pl.BlockSpec(memory_space=pl.ANY)] * (len(ins) + len(after)),
        out_specs=[pl.BlockSpec(memory_space=pl.ANY)] * len(outs),
        scratch_shapes=[pltpu.VMEM(array.shape, array.dtype) for array in arrays]
        + [pltpu.SemaphoreType.DMA((len(arrays),))],
        compiler_params=pltpu.CompilerParams(vmem_limit_bytes=SHARED_LIMIT),
    )(*ins, *after)


def split_kernel(*refs):
    lines, (own_ref, rest_ref) = refs[:4], refs[4:]
    split = own_ref.shape[2]
    for s, line in enumerate(lines):
        own_ref[s] = line[:, :split]
        rest_ref[s] = line[:, split:]


def split_column(lines, split):
    rows, cols = lines[0].shape
    outs = [shape_of((4, rows, part), BF16) for part in (split, cols - split)]
    return small_call(split_kernel, lines, (), outs)


def pack_kernel(*refs):
    ins, (shard_ref, feed_ref) = refs[:11], refs[11:]
    width = ins[0].shape[1]
    start = 0
    for line in (*ins[:3], ins[10], *ins[3:8]):
        shard_ref[:, start : start + line.shape[1]] = line[...]
        start += line.shape[1]
    for j in range(ins[8].shape[1] // width):
        feed_ref[16 * j : 16 * (j + 1), :] = ins[8][:, j * width : (j + 1) * width]
    feed_ref[64:, :] = ins[9][...]


def pack(weights, small):
    width = weights[0].shape[1]
    outs = [shape_of((16, 8 * width + LANES), BF16), shape_of((128, width), BF16)]
    return small_call(pack_kernel, (*map(in_hbm, weights), small), (), outs)


def memory_backward_kernel(memory_ref, grad_kv_ref, mem_ref, weight_ref, grad_memory_ref,
                           token_ref):
    mem_length = mem_ref.shape[1]
    width = memory_ref.shape[1]
    for first in range(0, width, 256):
        rows = slice(first, first + 256)
        grad_memory_ref[:, rows] = nt(
            grad_kv_ref[...], weight_ref[rows, 2 * width : 4 * width]
        ).astype(BF16)
    count = memory_ref.shape[0] // mem_length
    segments = step_rows(mem_ref, pl.program_id(0), count)
    columns = token_columns(segments)
    for r in range(count):
        rows = slice(r * mem_length, (r + 1) * mem_length)
        products = gram(memory_ref[rows, :]) * gram(grad_kv_ref[rows, :])
        token_ref[0, r : r + 1, :] = same_sum(products, segments, columns, r)


def gram_kernel(*refs):
    pairs, dec_ref, token_ref = refs[:-2], refs[-2], refs[-1]
    length = dec_ref.shape[1]
    count = pairs[0].shape[0] // length
    segments = step_rows(dec_ref, pl.program_id(0), count)
    columns = token_columns(segments)
    for r in range(count):
        rows = slice(r * length, (r + 1) * length)
        products = sum(
            gram(left[rows, :]) * gram(right[rows, :])
            for left, right in zip(pairs[::2], pairs[1::2])
        )
        token_ref[0, r : r + 1, :] = same_sum(products, segments, columns, r)


def rows_spec(array, steps):
    shape = (array.shape[0] // steps,) + array.shape[1:]
    return pl.BlockSpec(shape, lambda i, *_: (i,) + (0,) * (len(shape) - 1))


def whole_spec(array):
    return pl.BlockSpec(array.shape, lambda i, *_: (0,) * len(array.shape))


def in_hbm(array):
    return pltpu.with_memory_space_constraint(array, pltpu.HBM)


def ignoring(kernel, first, count):
    return lambda *refs: kernel(*refs[:first], *refs[first + count :])


def call(kernel, steps, me, blocked, whole, pieces, outs_blocked, outs_whole, scratch, flops,
         order, after=(), limit=VMEM_LIMIT):
    ins, in_specs = [], []
    blocked, whole = list(blocked), list(whole)
    for kind in order[0]:
        array = (blocked if kind == "i" else whole).pop(0)
        ins.append(array)
        in_specs.append(rows_spec(array, steps) if kind == "i" else whole_spec(array))
    ins = [in_hbm(array) for array in ins]
    kernel = ignoring(kernel, len(ins) + len(pieces) + (me is not None), len(after))
    ins += [*pieces, *after]
    in_specs += [pl.BlockSpec(memory_space=pl.ANY)] * (len(pieces) + len(after))
    outs, out_specs = [], []
    outs_blocked, outs_whole = list(outs_blocked), list(outs_whole)
    for kind in order[1]:
        out = (outs_blocked if kind == "i" else outs_whole).pop(0)
        outs.append(out)
        if kind == "a":
            out_specs.append(pl.BlockSpec(memory_space=pl.ANY))
        else:
            out_specs.append(rows_spec(out, steps) if kind == "i" else whole_spec(out))
    moved = sum(math.prod(a.shape) * a.dtype.itemsize for a in ins + outs)
    prefetch = 0 if me is None else 1
    return pl.pallas_call(
        kernel,
        out_shape=outs,
        grid_spec=pltpu.PrefetchScalarGridSpec(
            num_scalar_prefetch=prefetch,
            grid=(steps,),
            in_specs=in_specs,
            out_specs=out_specs,
            scratch_shapes=scratch,
        ),
        compiler_params=pltpu.CompilerParams(
            dimension_semantics=("arbitrary",), vmem_limit_bytes=limit
        ),
        cost_estimate=pl.CostEstimate(flops=flops, bytes_accessed=moved, transcendentals=0),
    )(*(() if me is None else (me,)), *ins)


FINE = ("z", "y", "core", "x")


def shape_of(shape, dtype):
    return jax.ShapeDtypeStruct(shape, dtype)


def kept(shape, dtype):
    return pltpu.HBM(shape, dtype)


def shift(array, mask):
    return lax.ppermute(array, FINE, [(i, i ^ mask) for i in range(32)])


def hold(array, after):
    return lax.optimization_barrier((array, after))[0]


def pack_feed(hidden, back):
    width = back.shape[1]
    hidden = hidden.reshape(-1, 16, 4, width).transpose(0, 2, 1, 3).reshape(-1, 64, width)
    return jnp.concatenate([hidden, back.reshape(-1, 64, width)], axis=1)


def unpack_feed(blocks):
    width = blocks.shape[2]
    hidden = blocks[:, :64].reshape(-1, 4, 16, width).transpose(0, 2, 1, 3)
    return hidden.reshape(-1, 4 * width), blocks[:, 64:].reshape(-1, width)


def small_row(gains, table):
    table = jnp.pad(table.reshape(-1, H), ((0, 0), (0, 16 - H)))
    row = jnp.concatenate([gain.reshape(-1, 16) for gain in gains] + [table], axis=1)
    row = jnp.pad(row, ((0, 0), (0, LANES - row.shape[1])))
    return jnp.pad(row[:, None], ((0, 0), (0, 15), (0, 0))).reshape(-1, LANES)


def in_order(slots):
    return slots[jnp.array([CODES.index(block) for block in range(32)])]


def as_rows(slots):
    return in_order(slots).reshape(-1, slots.shape[2]).astype(F32)


def shift_plane(pieces):
    return [shift(piece, mask) for piece, mask in zip(pieces, PLANE[1:])]


def shift_column(pieces):
    return [shift(piece, code) for piece, code in zip(pieces, COLUMN[1:])]


class Near:
    axes = FINE

    def __init__(self, weights):
        self.me = lax.axis_index(FINE)
        small = small_row(weights[10:13], weights[13])
        shard, feed = pack(weights[:10], small)
        self.feed = lax.all_gather(feed, FINE, axis=0)
        column = [shard, *shift_column([shard] * 3)]
        own, rest = split_column(column, 3 * weights[0].shape[1] + LANES)
        plane = [own, *shift_plane([own] * 3)]
        self.plane = [rest, *shift_plane([rest] * 3)]
        self.own = plane + [shift(piece, 2) for piece in plane]

    def cross(self, after):
        plane = [hold(piece, after) for piece in self.plane]
        return plane + [shift(piece, 2) for piece in plane]

    def feed_core(self, slots):
        return lax.psum_scatter(slots.reshape((2, 4, 4) + slots.shape[1:]), "core")

    def feed_plane(self, slots):
        return lax.psum_scatter(slots, ("y", "x"))

    def feed_column(self, slots):
        return lax.psum_scatter(slots, "z")


class Far:
    axes = ("wide", "narrow")
    me = 0

    def __init__(self, weights):
        weights = [lax.all_gather(w, self.axes, axis=0, tiled=True) for w in weights]
        self.take(weights)

    def take(self, weights):
        self.own = self.pieces(*weights[:3], small_row(weights[10:13], weights[13]))
        self.rest = self.pieces(*weights[3:8])
        self.feed = pack_feed(weights[8], weights[9])

    def pieces(self, *parts):
        blocks = jnp.concatenate(parts, axis=1).reshape(32, 16, -1)[jnp.array(CODES)]
        return [blocks[4 * t : 4 * t + 4] for t in range(8)]

    def cross(self, after):
        return self.rest

    def feed_core(self, slots):
        return slots

    feed_plane = feed_column = feed_core


def on_device(near, tokens, memory, cotangent, dec_segments, mem_segments, padding, buckets,
              *weights):
    way = (Near if near else Far)(weights)
    result, grad_tokens, grad_memory, grads, examples, square = local_part(
        way, tokens, memory, cotangent, dec_segments, mem_segments, padding, buckets
    )
    if near:
        sent = lax.all_to_all(square, FINE, 0, 0, tiled=True)
        global_norm = jnp.sum(sent[:, 0])
    else:
        grads = [lax.psum_scatter(g, way.axes, scatter_dimension=0, tiled=True) for g in grads]
        global_norm = lax.psum(sum(jnp.sum(g * g) for g in grads), way.axes)
    return (result, grad_tokens, grad_memory, *grads, examples, global_norm / COUNT)


def local_part(way, tokens, memory, cotangent, dec_segments, mem_segments, padding, buckets):
    seqs, length, width = tokens.shape
    mem_length = memory.shape[1]
    steps = seqs // STEP_ROWS
    small_steps = seqs // SMALL_ROWS
    dec, mem = seqs * length, seqs * mem_length
    step_dec = STEP_ROWS * length
    ff = 4 * width

    buckets = buckets[None]
    tokens2, memory2, cotangent2 = (
        array.reshape(-1, width) for array in (tokens, memory, cotangent)
    )
    dma = pltpu.SemaphoreType.DMA

    me = jnp.full((1,), way.me, jnp.int32)
    flops = 2 * dec * width * width

    input_a, qkv_a, prob_a, attended_a, self_w, gains = call(
        self_forward_kernel, small_steps, me, (tokens2,), (dec_segments, padding, buckets), way.own,
        (
            kept((dec, width), BF16),
            kept((dec, 3 * width), BF16),
            kept((seqs, PAIRS, length, 2 * length), BF16),
            kept((dec, width), BF16),
        ),
        (kept((width, 3 * width), BF16), kept((8, width), F32)),
        [pltpu.VMEM((PAIRS, length, 2 * length), F32), pltpu.VMEM((width, LANES), BF16), dma((64,))],
        6 * flops, ("iwww", "iiiiww"), (), SHARED_LIMIT,
    )
    kv_b, cross_w = call(
        memory_forward_kernel, small_steps, me, (memory2,), (), way.cross(attended_a),
        (kept((mem, 2 * width), BF16),), (kept((width, 5 * width), BF16),), [dma((32,))],
        4 * flops, ("i", "iw"), (), SHARED_LIMIT,
    )
    middle, input_b, query_b, prob_b, attended_b, after_cross = call(
        cross_forward_kernel, small_steps, None, (tokens2, attended_a, kv_b),
        (dec_segments, mem_segments, gains, cross_w), (),
        (
            kept((dec, width), BF16),
            kept((dec, width), BF16),
            kept((dec, width), BF16),
            kept((seqs, PAIRS, mem_length, 2 * length), BF16),
            kept((dec, width), BF16),
            kept((dec, width), BF16),
        ),
        (), [], 6 * flops, ("iiiwwww", "iiiiii"),
    )
    total, square = kept((1, width), F32), shape_of((steps, 4 * STEP_ROWS, LANES), F32)
    token_shape = shape_of((steps, 8, length), F32)
    small_token = shape_of((small_steps, 8, length), F32)
    result, branch_b, feed_slots, gain_c, square_c, token_c = call(
        feed_kernel, ff // width, None, (),
        (after_cross, cotangent2, dec_segments, padding, gains), (way.feed,), (),
        (
            shape_of((dec, width), BF16),
            kept((dec, width), BF16),
            shape_of((32, 128, width), BF16),
            total,
            square,
            token_shape,
        ),
        [
            pltpu.VMEM((32, 16, ff), BF16),
            pltpu.VMEM((32, 64, width), BF16),
            *[pltpu.VMEM((dec, width), BF16)] * 2,
            *[pltpu.VMEM((width, dec), BF16)] * 2,
            *[pltpu.VMEM((dec, ff), BF16)] * 2,
            pltpu.VMEM((32, 16, width), BF16),
            pltpu.VMEM((8, 64, width), BF16),
            dma((4, 2)),
            dma((9,)),
        ],
        26 * flops, ("wwwww", "wwawww"),
    )
    feed_sum = way.feed_core(feed_slots)
    slot = shape_of((16, 16, 5 * width), BF16)
    grad_query_b, grad_kv_b, branch_a, cross_low, cross_high, gain_b, square_b = call(
        cross_backward_kernel, steps, me,
        (branch_b, middle, memory2, attended_a, input_b, query_b, kv_b, prob_b, attended_b),
        (dec_segments, gains, cross_w), (),
        (
            kept((dec, width), BF16),
            kept((mem, 2 * width), BF16),
            kept((dec, width), BF16),
            square,
        ),
        (kept(slot.shape, BF16), slot, total),
        [pltpu.VMEM((width, 5 * width), F32), pltpu.VMEM((step_dec, width), BF16)],
        20 * flops, ("iiiiiiiiiwww", "iiiwwwi"),
    )
    feed_sum = way.feed_plane(hold(feed_sum, grad_query_b))
    near = isinstance(way, Near)
    if near:
        sent = shift(cross_high, 2)
    grad_qkv_a, table, table_square = call(
        self_scores_kernel, steps, None, (branch_a, qkv_a, prob_a),
        (dec_segments, buckets, cross_w), (),
        (kept((dec, 3 * width), BF16), shape_of((steps, STEP_ROWS, 8, LANES), F32)),
        (kept((H, LANES), F32),),
        [pltpu.VMEM((step_dec, width), BF16), pltpu.VMEM((STEP_ROWS, H, 8, length), F32)],
        10 * flops, ("iiiwww", "iwi"),
    )
    waits = ()
    if near:
        cross_parts = pair_sum(cross_low, sent, (grad_qkv_a,))
        crossed = shift_plane(cross_parts[1:])
        waits = (cross_parts[0],)
    slot = shape_of((16, 16, 3 * width + LANES), BF16)
    grad_tokens, self_low, self_high, square_a = call(
        self_weights_kernel, steps, me, (branch_a, tokens2, input_a, grad_qkv_a),
        (dec_segments, gains, self_w, table, gain_b, gain_c), (),
        (shape_of((dec, width), BF16), square),
        (kept(slot.shape, BF16), slot),
        [
            pltpu.VMEM((width, 3 * width), F32),
            pltpu.VMEM((1, width), F32),
            pltpu.VMEM((width, LANES), F32),
        ],
        7 * flops, ("iiiiwwwwww", "iwwi"), waits,
    )

    def grams(pairs, *after):
        (tokens_part,) = call(
            gram_kernel, small_steps, None, pairs, (dec_segments,), (), (small_token,), (), [],
            2 * flops, ("i" * len(pairs) + "w", "i"), after, SHARED_LIMIT,
        )
        return tokens_part

    def fill_cross(*after):
        return grams((input_b, grad_query_b, attended_b, branch_b), *after)

    def fill_self(*after):
        return grams((input_a, grad_qkv_a, attended_a, branch_a), *after)

    def fill_memory(*after):
        return call(
            memory_backward_kernel, small_steps, None, (memory2, grad_kv_b),
            (mem_segments, cross_w), (),
            (shape_of((mem, width), BF16), shape_of((small_steps, 8, mem_length), F32)), (), [],
            10 * flops, ("iiww", "ii"), after, SHARED_LIMIT,
        )

    if near:
        sent = shift(hold(self_high, crossed[0]), 2)
        token_b = fill_cross(self_low)
        self_parts = pair_sum(self_low, sent, (token_b,))
        self_sent = shift_plane(self_parts[1:])
        feed_sum = hold(feed_sum, token_b)
        token_a = fill_self(self_parts[0], feed_sum)
        feed_sum = way.feed_column(feed_sum)
        groups = [[self_parts[0], *self_sent], [cross_parts[0], *crossed]]
        own, *rest = plane_sum(groups, (token_a,))
        line_sent = shift_column(rest)
        grad_memory, token_m = fill_memory(own)
        feed_sum = hold(feed_sum, token_m).reshape(128, width)
        grad_hidden, grad_back, square = small_call(
            feed_end_kernel, (feed_sum,), (token_m,),
            [shape_of((16, ff), F32), shape_of((64, width), F32), shape_of((8, LANES), F32)],
        )
        line = shape_of((slot.shape[1], width), F32)
        *parts, square = small_call(
            column_end_kernel, (own, *line_sent, square), (token_m,),
            [line] * 3 + [shape_of((16, LANES), F32)] + [line] * 5 + [shape_of((32, LANES), F32)],
        )
        self_grads, small, cross_grads = parts[:3], parts[3], parts[4:]
        token_m = hold(token_m, square)
    else:
        token_b, token_a = fill_cross(), fill_self()
        grad_memory, token_m = fill_memory()
        cross_sum = as_rows(jnp.concatenate([cross_low, cross_high]))
        self_sum = as_rows(jnp.concatenate([self_low, self_high]))
        cross_grads = [cross_sum[:, k * width : (k + 1) * width] for k in range(5)]
        self_grads = [self_sum[:, k * width : (k + 1) * width] for k in range(3)]
        small = self_sum[:, 3 * width :]
        grad_hidden, grad_back = unpack_feed(in_order(feed_sum).astype(F32))
        square = None
    grads = self_grads + cross_grads + [grad_hidden, grad_back]
    grads += [small[:, k] for k in range(3)]
    grads.append(small[:, 3].reshape(-1, 16)[:, :H].reshape(-1))

    def row_parts(parts, count):
        return parts[:, :count].reshape(seqs, -1)

    def by_example(part, segments):
        hits = segments[:, None, :] == lax.broadcasted_iota(jnp.int32, (1, NSEG, 1), 1)
        return jnp.sum(jnp.where(hits, part[:, None, :], 0.0), axis=-1)

    token_d = row_parts(token_a + token_b, SMALL_ROWS) + row_parts(token_c, STEP_ROWS)
    examples = by_example(token_d, dec_segments)
    examples = examples + by_example(row_parts(token_m, SMALL_ROWS), mem_segments)
    squares = (square_a + square_b + square_c)[:, :, 0].reshape(seqs, NSEG)
    examples = examples + squares + table_square[..., :NSEG, 0].reshape(seqs, NSEG)
    return (
        result.reshape(tokens.shape),
        grad_tokens.reshape(tokens.shape),
        grad_memory.reshape(memory.shape),
        grads,
        examples / COUNT,
        square,
    )


def solution(mesh):
    near = tuple(mesh.shape.values()) == (16, 2)
    if near:
        mesh = jax.sharding.Mesh(mesh.devices.reshape(4, 2, 2, 2), FINE)
    axes = tuple(mesh.axis_names)
    rows = P(axes)
    arrays, weights, vectors = (P(axes, None, None),) * 3, (P(axes, None),) * 10, (rows,) * 4
    placed = arrays + (P(axes, None),) * 3 + (P(),) + weights + vectors
    return jax.shard_map(
        partial(on_device, near),
        mesh=mesh,
        in_specs=placed,
        out_specs=arrays + weights + vectors + (P(axes, None), P()),
        check_vma=False,
    )
```

profile of v0, /device:TPU:0, one launch (start us, length us, event | category | flops | bytes accessed | tf_op | source)
XLA Modules:
  0.0 265.1 jit_solution(4493063154884751810)
XLA Ops:
  7.2 0.8 fusion.2
  8.0 2.0 shard_map.348
  10.1 5.1 %collective-permute-start.2 = (bf16[16,4224]{1,0:T(8,128)(2,1)S(1)}, bf16[16,4224]{1,0:T(8,128)(2,1)S(1)}, u32[]{:S(2)}, u32[]{:S(2)}) collective-permute-start(bf16[16,4224]{1,0:T(8,128)(2,1)S(1)} %get-tuple-element.93.refs_0_), channel_id=1, source_target_pairs={{0,24},{1,25},{2,26},{3,27},{4,28},{5,29},{6,30},{7,31},{8,16},{9,... | collective-permute-start | bytes 405512 | tf_op jit(solution)/shard_map/ppermute | solution.py:821
  15.2 0.6 collective-permute-start
  15.8 3.9 %collective-permute-done.2.refs_3_ = bf16[16,4224]{1,0:T(8,128)(2,1)S(1)} collective-permute-done((bf16[16,4224]{1,0:T(8,128)(2,1)S(1)}, bf16[16,4224]{1,0:T(8,128)(2,1)S(1)}, u32[]{:S(2)}, u32[]{:S(2)}) %collective-permute-start.2) | collective-permute-done | bytes 135200 | tf_op jit(solution)/shard_map/ppermute | solution.py:821
  19.7 7.0 %collective-permute-done.1.refs_2_ = bf16[16,4224]{1,0:T(8,128)(2,1)S(1)} collective-permute-done((bf16[16,4224]{1,0:T(8,128)(2,1)S(1)}, bf16[16,4224]{1,0:T(8,128)(2,1)S(1)}, u32[]{:S(2)}, u32[]{:S(2)}) %collective-permute-start.1) | collective-permute-done | bytes 135200 | tf_op jit(solution)/shard_map/ppermute | solution.py:821
  26.7 1.1 shard_map.349
  27.9 2.5 collective-permute-start.5
  31.4 5.6 %collective-permute-done.5.refs_8_ = bf16[4,16,1664]{2,1,0:T(8,128)(2,1)S(1)} collective-permute-done((bf16[4,16,1664]{2,1,0:T(8,128)(2,1)S(1)}, bf16[4,16,1664]{2,1,0:T(8,128)(2,1)S(1)}, u32[]{:S(2)}, u32[]{:S(2)}) %collective-permute-start.5) | collective-permute-done | bytes 213024 | tf_op jit(solution)/shard_map/ppermute | solution.py:821
  37.0 2.6 collective-permute-done.4.refs_7_
  40.1 1.7 collective-permute-start.12
  41.9 1.2 collective-permute-start.11
  43.1 0.5 collective-permute-start.10
  43.6 11.6 %shard_map.350 = (bf16[1536,512]{1,0:T(8,128)(2,1)}, bf16[1536,1536]{1,0:T(8,128)(2,1)}, bf16[12,4,128,256]{3,2,1,0:T(8,128)(2,1)}, bf16[1536,512]{1,0:T(8,128)(...) custom-call(s32[1]{0:T(128)} %bitcast.1.refs_0_, bf16[1536,512]{1,0:T(8,128)(2,1)} %bitcast.45, s32[12,128]{1,0:T(8,128)} %refs_4_.7, ...), custom_call_target="tpu_custom_call" | custom-call | flops 4831838208 | bytes 15888896 | tf_op jit(solution)/shard_map/pallas_call | solution.py:792
  55.3 2.7 %collective-permute-done.11.refs_4_ = bf16[4,16,2560]{2,1,0:T(8,128)(2,1)S(1)} collective-permute-done((bf16[4,16,2560]{2,1,0:T(8,128)(2,1)S(1)}, bf16[4,16,2560]{2,1,0:T(8,128)(2,1)S(1)}, u32[]{:S(2)}, u32[]{:S(2)}) %collective-permute-start.11) | collective-permute-done | bytes 327712 | tf_op jit(solution)/shard_map/ppermute | solution.py:821
  58.0 1.6 collective-permute-done.10.refs_3_
  60.6 0.6 collective-permute-done.13.refs_6_
  62.7 11.3 %shard_map.351 = (bf16[3072,1024]{1,0:T(8,128)(2,1)}, bf16[512,2560]{1,0:T(8,128)(2,1)}) custom-call(s32[1]{0:T(128)} %bitcast.1.refs_0_, bf16[3072,512]{1,0:T(8,128)(2,1)} %bitcast.41, bf16[4,16,2560]{2,1,0:T(8,128)(2,1)S(1)} %get-tuple-element.97.refs_2_, bf16[4,16,2560]{2,1,0:T(8,128)(2,1)S(1)} %collective-permute-done.10.refs_3_, ...), custom_call_target="tpu_custom_call" | custom-call | flops 3221225472 | bytes 14680064 | tf_op jit(solution)/shard_map/pallas_call | solution.py:792
  74.0 17.1 %shard_map.352 = (bf16[1536,512]{1,0:T(8,128)(2,1)}, bf16[1536,512]{1,0:T(8,128)(2,1)}, bf16[1536,512]{1,0:T(8,128)(2,1)}, bf16[12,4,256,256]{3,2,1,0:T(8,128)(2...) custom-call(bf16[1536,512]{1,0:T(8,128)(2,1)} %bitcast.46, ...), custom_call_target="tpu_custom_call" | custom-call | flops 4831838208 | bytes 26249216 | tf_op jit(solution)/shard_map/pallas_call | solution.py:792
  91.1 48.7 %shard_map.353 = (bf16[1536,512]{1,0:T(8,128)(2,1)}, bf16[1536,512]{1,0:T(8,128)(2,1)}, bf16[32,128,512]{2,1,0:T(8,128)(2,1)}, f32[1,512]{1,0:T(1,128)}, f32[3,16,128]{2,1,0:T(8,128)}, /*index=5*/f32[3,8,128]{2,1,0:T(8,128)}) custom-call(bf16[1536,512]{1,0:T(8,128)(2,1)} %get-tuple-element.104.refs_0_, bf16[1536,512]{1,0:T(8,128)(2,1)} %bitcast.44, ...), custom_call_target="tpu_custom_call" | custom-call | flops 20937965568 | bytes 14747648 | tf_op jit(solution)/shard_map/pallas_call | solution.py:792
  139.9 24.7 %shard_map.354 = (bf16[1536,512]{1,0:T(8,128)(2,1)}, bf16[3072,1024]{1,0:T(8,128)(2,1)}, bf16[1536,512]{1,0:T(8,128)(2,1)}, bf16[16,16,2560]{2,1,0:T(8,128)(2,1)...) custom-call(s32[1]{0:T(128)} %bitcast.1.refs_0_, ...), custom_call_target="tpu_custom_call" | custom-call | flops 16106127360 | bytes 39895040 | tf_op jit(solution)/shard_map/pallas_call | solution.py:792
  164.7 1.2 copy-done.12
  166.0 13.5 %shard_map.355 = (bf16[1536,1536]{1,0:T(8,128)(2,1)}, f32[8,128]{1,0:T(8,128)}, f32[3,4,8,128]{3,2,1,0:T(8,128)}) custom-call(bf16[1536,512]{1,0:T(8,128)(2,1)} %get-tuple-element.113.refs_0_.refs_1_.refs_3_, bf16[1536,1536]{1,0:T(8,128)(2,1)} %get-tuple-element.115.refs_1_, bf16[12,4,128,256]{3,2,1,0:T(8,128)(2,1)} %get-tuple-element.116.refs_2_, ...), custom_call_target="tpu_custom_call" | custom-call | flops 8053063680 | bytes 16837120 | tf_op jit(solution)/shard_map/pallas_call | solution.py:792
  179.5 1.8 shard_map.356
  181.4 0.7 copy-done.2
  182.4 11.7 %shard_map.357 = (bf16[1536,512]{1,0:T(8,128)(2,1)}, bf16[16,16,1664]{2,1,0:T(8,128)(2,1)}, bf16[16,16,1664]{2,1,0:T(8,128)(2,1)}, f32[3,16,128]{2,1,0:T(8,128)}) custom-call(s32[1]{0:T(128)} %bitcast.1.refs_0_, bf16[1536,512]{1,0:T(8,128)(2,1)} %get-tuple-element.113.refs_0_.refs_1_.refs_3_, bf16[1536,512]{1,0:T(8,128)(2,1)} %bitcast.47, ...), custom_call_target="tpu_custom_call" | custom-call | flops 5637144576 | bytes 14669824 | tf_op jit(solution)/shard_map/pallas_call | solution.py:792
  194.4 1.9 collective-permute-start.23
  196.3 1.4 collective-permute-start.24
  197.7 1.2 copy-done
  198.9 4.5 %shard_map.358.refs_2_ = f32[3,8,128]{2,1,0:T(8,128)S(1)} custom-call(bf16[1536,512]{1,0:T(8,128)(2,1)} %get-tuple-element.109.refs_5_.refs_0_, bf16[1536,512]{1,0:T(8,128)(2,1)} %get-tuple-element.131.refs_1_, bf16[1536,512]{1,0:T(8,128)(2,1)} %get-tuple-element.112.refs_9_.refs_2_, bf16[1536,512]{1,0:T(8,128)(2,1)} %get-tuple-element.107.refs_1_.refs_3_, ...), custom_call_target="tpu_custom_call" | custom-call | flops 1610612736 | bytes 7161856 | tf_op jit(solution)/shard_map/pallas_call | solution.py:792
  203.5 2.3 shard_map.359
  206.1 1.9 collective-permute-start.21
  208.0 1.4 collective-permute-start.22
  209.9 1.0 copy-done.1
  211.0 6.0 %shard_map.360.refs_8_ = f32[3,8,128]{2,1,0:T(8,128)S(1)} custom-call(bf16[1536,512]{1,0:T(8,128)(2,1)} %get-tuple-element.114.refs_3_.refs_0_, bf16[1536,1536]{1,0:T(8,128)(2,1)} %get-tuple-element.117.refs_2_.refs_4_.refs_1_, bf16[1536,512]{1,0:T(8,128)(2,1)} %get-tuple-element.95.refs_1_.refs_4_.refs_2_, ...), custom_call_target="tpu_custom_call" | custom-call | flops 1610612736 | bytes 10192896 | tf_op jit(solution)/shard_map/pallas_call | solution.py:792
  217.0 5.7 %collective-permute-done.21.refs_2_ = bf16[4,16,1664]{2,1,0:T(8,128)(2,1)S(1)} collective-permute-done((bf16[4,16,1664]{2,1,0:T(8,128)(2,1)S(1)}, bf16[4,16,1664]{2,1,0:T(8,128)(2,1)S(1)}, u32[]{:S(2)}, u32[]{:S(2)}) %collective-permute-start.21) | collective-permute-done | bytes 213024 | tf_op jit(solution)/shard_map/ppermute | solution.py:821
  222.8 2.4 shard_map.361
  225.2 1.6 collective-permute-start.25
  226.7 2.4 collective-permute-start.26
  229.7 10.1 %shard_map.362 = (bf16[3072,512]{1,0:T(8,128)(2,1)}, f32[3,8,256]{2,1,0:T(8,128)S(1)}) custom-call(bf16[3072,512]{1,0:T(8,128)(2,1)} %bitcast.43, bf16[3072,1024]{1,0:T(8,128)(2,1)} %get-tuple-element.126.refs_1_, s32[12,256]{1,0:T(8,128)} %refs_2_.7, bf16[512,2560]{1,0:T(8,128)(2,1)} %get-tuple-element.103.refs_6_.refs_12_.refs_5_.refs_3_, ...), custom_call_target="tpu_custom_call" | custom-call | flops 8053063680 | bytes 15511552 | tf_op jit(solution)/shard_map/pallas_call | solution.py:792
  239.9 0.9 copy-done.4
  240.8 0.9 shard_map.363
  241.7 1.6 shard_map.364
  243.4 0.7 slice_reduce_fusion.2
  244.2 4.6 %all-to-all-start = ((f32[32,1,128]{2,1,0:T(1,128)}), f32[32,1,128]{2,1,0:T(1,128)S(1)}, u32[]{:S(2)}, u32[]{:S(2)}) async-start(f32[32,1,128]{2,1,0:T(1,128)} %bitcast.22), calls=%async_computation.2 | async-start | bytes 32768 | tf_op jit(solution)/shard_map/all_to_all | solution.py:924
  249.3 0.7 copy.53
  250.0 6.0 %all-to-all-done = f32[32,1,128]{2,1,0:T(1,128)S(1)} async-done(((f32[32,1,128]{2,1,0:T(1,128)}), f32[32,1,128]{2,1,0:T(1,128)S(1)}, u32[]{:S(2)}, u32[]{:S(2)}) %all-to-all-start) | async-done | bytes 16416 | tf_op jit(solution)/shard_map/all_to_all | solution.py:924
  256.0 0.6 slice_reduce_fusion.1
  (83 shorter events, 7.2 us)
Async XLA Ops:
  7.2 83.9 %all-gather.3.cloned.1.call-start = ((), (), s32[]{:S(2)}) async-start(), calls=%async_computation.6 | async-start | bytes 4325376 | tf_op jit(solution)/shard_map/all_gather | solution.py:870
  10.0 154.6 %reduce-scatter.6.cloned.1.call-start = ((), (), s32[]{:S(2)}) async-start(), calls=%async_computation.4 | async-start | bytes 6291456 | tf_op jit(solution)/shard_map/reduce_scatter | solution.py:882
  10.1 9.6 %collective-permute-start.2 = (bf16[16,4224]{1,0:T(8,128)(2,1)S(1)}, bf16[16,4224]{1,0:T(8,128)(2,1)S(1)}, u32[]{:S(2)}, u32[]{:S(2)}) collective-permute-start(bf16[16,4224]{1,0:T(8,128)(2,1)S(1)} %get-tuple-element.93.refs_0_), channel_id=1, source_target_pairs={{0,24},{1,25},{2,26},{3,27},{4,28},{5,29},{6,30},{7,31},{8,16},{9,... | collective-permute-start | bytes 405512 | tf_op jit(solution)/shard_map/ppermute | solution.py:821
  15.2 11.5 %collective-permute-start.1 = (bf16[16,4224]{1,0:T(8,128)(2,1)S(1)}, bf16[16,4224]{1,0:T(8,128)(2,1)S(1)}, u32[]{:S(2)}, u32[]{:S(2)}) collective-permute-start(bf16[16,4224]{1,0:T(8,128)(2,1)S(1)} %get-tuple-element.93.refs_0_), channel_id=1, source_target_pairs={{0,16},{1,17},{2,18},{3,19},{4,20},{5,21},{6,22},{7,23},{8,24},{9,... | collective-permute-start | bytes 405512 | tf_op jit(solution)/shard_map/ppermute | solution.py:821
  15.2 11.5 %collective-permute-start = (bf16[16,4224]{1,0:T(8,128)(2,1)S(1)}, bf16[16,4224]{1,0:T(8,128)(2,1)S(1)}, u32[]{:S(2)}, u32[]{:S(2)}) collective-permute-start(bf16[16,4224]{1,0:T(8,128)(2,1)S(1)} %get-tuple-element.93.refs_0_), channel_id=1, source_target_pairs={{0,8},{1,9},{2,10},{3,11},{4,12},{5,13},{6,14},{7,15},{8,0},{9,1},... | collective-permute-start | bytes 405512 | tf_op jit(solution)/shard_map/ppermute | solution.py:821
  27.9 9.2 %collective-permute-start.5 = (bf16[4,16,1664]{2,1,0:T(8,128)(2,1)S(1)}, bf16[4,16,1664]{2,1,0:T(8,128)(2,1)S(1)}, u32[]{:S(2)}, u32[]{:S(2)}) collective-permute-start(bf16[4,16,1664]{2,1,0:T(8,128)(2,1)S(1)} %get-tuple-element.94.refs_5_), channel_id=1, source_target_pairs={{0,5},{1,4},{2,7},{3,6},{4,1},{5,0},{6,3},{7,2},{8,13},{9,12},{10,... | collective-permute-start | bytes 638984 | tf_op jit(solution)/shard_map/ppermute | solution.py:821
  30.4 9.2 %collective-permute-start.4 = (bf16[4,16,1664]{2,1,0:T(8,128)(2,1)S(1)}, bf16[4,16,1664]{2,1,0:T(8,128)(2,1)S(1)}, u32[]{:S(2)}, u32[]{:S(2)}) collective-permute-start(bf16[4,16,1664]{2,1,0:T(8,128)(2,1)S(1)} %get-tuple-element.94.refs_5_), channel_id=1, source_target_pairs={{0,4},{1,5},{2,6},{3,7},{4,0},{5,1},{6,2},{7,3},{8,12},{9,13},{10,... | collective-permute-start | bytes 638984 | tf_op jit(solution)/shard_map/ppermute | solution.py:821
  30.9 8.8 %collective-permute-start.3 = (bf16[4,16,1664]{2,1,0:T(8,128)(2,1)S(1)}, bf16[4,16,1664]{2,1,0:T(8,128)(2,1)S(1)}, u32[]{:S(2)}, u32[]{:S(2)}) collective-permute-start(bf16[4,16,1664]{2,1,0:T(8,128)(2,1)S(1)} %get-tuple-element.94.refs_5_), channel_id=1, source_target_pairs={{0,1},{1,0},{2,3},{3,2},{4,5},{5,4},{6,7},{7,6},{8,9},{9,8},{10,11... | collective-permute-start | bytes 638984 | tf_op jit(solution)/shard_map/ppermute | solution.py:821
  31.4 10.4 %collective-permute-start.6 = (bf16[4,16,1664]{2,1,0:T(8,128)(2,1)S(1)}, bf16[4,16,1664]{2,1,0:T(8,128)(2,1)S(1)}, u32[]{:S(2)}, u32[]{:S(2)}) collective-permute-start(bf16[4,16,1664]{2,1,0:T(8,128)(2,1)S(1)} %get-tuple-element.94.refs_5_), channel_id=1, source_target_pairs={{0,2},{1,3},{2,0},{3,1},{4,6},{5,7},{6,4},{7,5},{8,10},{9,11},{10,... | collective-permute-start | bytes 638984 | tf_op jit(solution)/shard_map/ppermute | solution.py:821
  37.0 6.1 %collective-permute-start.9 = (bf16[4,16,1664]{2,1,0:T(8,128)(2,1)S(1)}, bf16[4,16,1664]{2,1,0:T(8,128)(2,1)S(1)}, u32[]{:S(2)}, u32[]{:S(2)}) collective-permute-start(bf16[4,16,1664]{2,1,0:T(8,128)(2,1)S(1)} %collective-permute-done.5.refs_8_), channel_id=1, source_target_pairs={{0,2},{1,3},{2,0},{3,1},{4,6},{5,7},{6,4},{7,5},{8,10},{9,11},{10,... | collective-permute-start | bytes 638984 | tf_op jit(solution)/shard_map/ppermute | solution.py:821
  39.6 4.0 %collective-permute-start.8 = (bf16[4,16,1664]{2,1,0:T(8,128)(2,1)S(1)}, bf16[4,16,1664]{2,1,0:T(8,128)(2,1)S(1)}, u32[]{:S(2)}, u32[]{:S(2)}) collective-permute-start(bf16[4,16,1664]{2,1,0:T(8,128)(2,1)S(1)} %collective-permute-done.4.refs_7_), channel_id=1, source_target_pairs={{0,2},{1,3},{2,0},{3,1},{4,6},{5,7},{6,4},{7,5},{8,10},{9,11},{10,... | collective-permute-start | bytes 638984 | tf_op jit(solution)/shard_map/ppermute | solution.py:821
  39.7 3.9 %collective-permute-start.7 = (bf16[4,16,1664]{2,1,0:T(8,128)(2,1)S(1)}, bf16[4,16,1664]{2,1,0:T(8,128)(2,1)S(1)}, u32[]{:S(2)}, u32[]{:S(2)}) collective-permute-start(bf16[4,16,1664]{2,1,0:T(8,128)(2,1)S(1)} %collective-permute-done.3.refs_6_), channel_id=1, source_target_pairs={{0,2},{1,3},{2,0},{3,1},{4,6},{5,7},{6,4},{7,5},{8,10},{9,11},{10,... | collective-permute-start | bytes 638984 | tf_op jit(solution)/shard_map/ppermute | solution.py:821
  40.1 15.1 %collective-permute-start.12 = (bf16[4,16,2560]{2,1,0:T(8,128)(2,1)S(1)}, bf16[4,16,2560]{2,1,0:T(8,128)(2,1)S(1)}, u32[]{:S(2)}, u32[]{:S(2)}) collective-permute-start(bf16[4,16,2560]{2,1,0:T(8,128)(2,1)S(1)} %get-tuple-element.97.refs_2_), channel_id=1, source_target_pairs={{0,5},{1,4},{2,7},{3,6},{4,1},{5,0},{6,3},{7,2},{8,13},{9,12},{10,... | collective-permute-start | bytes 983048 | tf_op jit(solution)/shard_map/ppermute | solution.py:821
  41.9 16.1 %collective-permute-start.11 = (bf16[4,16,2560]{2,1,0:T(8,128)(2,1)S(1)}, bf16[4,16,2560]{2,1,0:T(8,128)(2,1)S(1)}, u32[]{:S(2)}, u32[]{:S(2)}) collective-permute-start(bf16[4,16,2560]{2,1,0:T(8,128)(2,1)S(1)} %get-tuple-element.97.refs_2_), channel_id=1, source_target_pairs={{0,4},{1,5},{2,6},{3,7},{4,0},{5,1},{6,2},{7,3},{8,12},{9,13},{10,... | collective-permute-start | bytes 983048 | tf_op jit(solution)/shard_map/ppermute | solution.py:821
  43.1 16.5 %collective-permute-start.10 = (bf16[4,16,2560]{2,1,0:T(8,128)(2,1)S(1)}, bf16[4,16,2560]{2,1,0:T(8,128)(2,1)S(1)}, u32[]{:S(2)}, u32[]{:S(2)}) collective-permute-start(bf16[4,16,2560]{2,1,0:T(8,128)(2,1)S(1)} %get-tuple-element.97.refs_2_), channel_id=1, source_target_pairs={{0,1},{1,0},{2,3},{3,2},{4,5},{5,4},{6,7},{7,6},{8,9},{9,8},{10,11... | collective-permute-start | bytes 983048 | tf_op jit(solution)/shard_map/ppermute | solution.py:821
  59.6 1.6 collective-permute-start.13
  59.6 2.1 collective-permute-start.14
  60.1 2.1 collective-permute-start.15
  60.1 2.5 collective-permute-start.16
  139.9 70.0 %reduce-scatter.10.cloned.1.call-start = ((), (), s32[]{:S(2)}) async-start(), calls=%async_computation.7 | async-start | bytes 2621440
  164.6 1.3 copy-start.12
  164.6 75.3 %reduce-scatter.8.cloned.1.call-start = ((), (), s32[]{:S(2)}) async-start(), calls=%async_computation.5 | async-start | bytes 655360 | tf_op jit(solution)/shard_map/reduce_scatter | solution.py:888
  165.9 13.6 %collective-permute-start.17 = (bf16[16,16,2560]{2,1,0:T(8,128)(2,1)S(1)}, bf16[16,16,2560]{2,1,0:T(8,128)(2,1)S(1)}, u32[]{:S(2)}, u32[]{:S(2)}) collective-permute-start(bf16[16,16,2560]{2,1,0:T(8,128)(2,1)S(1)} %copy-done.12), channel_id=1, source_target_pairs={{0,2},{1,3},{2,0},{3,1},{4,6},{5,7},{6,4},{7,5},{8,10},{9,11},{10,... | collective-permute-start | bytes 3932168 | tf_op jit(solution)/shard_map/ppermute | solution.py:821
  181.3 0.7 copy-start.2
  182.1 12.1 %collective-permute-start.18 = (bf16[4,16,2560]{2,1,0:T(8,128)(2,1)S(1)}, bf16[4,16,2560]{2,1,0:T(8,128)(2,1)S(1)}, u32[]{:S(2)}, u32[]{:S(2)}) collective-permute-start(bf16[4,16,2560]{2,1,0:T(8,128)(2,1)S(1)} %get-tuple-element.129), channel_id=1, source_target_pairs={{0,1},{1,0},{2,3},{3,2},{4,5},{5,4},{6,7},{7,6},{8,9},{9,8},{10,11... | collective-permute-start | bytes 983048 | tf_op jit(solution)/shard_map/ppermute | solution.py:821
  182.4 11.9 %copy-start.10 = (f32[3,4,8,128]{3,2,1,0:T(8,128)S(1)}, f32[3,4,8,128]{3,2,1,0:T(8,128)}, u32[]{:S(2)}) copy-start(f32[3,4,8,128]{3,2,1,0:T(8,128)} %get-tuple-element.166) | copy-start | bytes 147460
  194.2 9.3 %collective-permute-start.19 = (bf16[16,16,1664]{2,1,0:T(8,128)(2,1)}, bf16[16,16,1664]{2,1,0:T(8,128)(2,1)S(1)}, u32[]{:S(2)}, u32[]{:S(2)}) collective-permute-start(bf16[16,16,1664]{2,1,0:T(8,128)(2,1)} %get-tuple-element.130), channel_id=1, source_target_pairs={{0,2},{1,3},{2,0},{3,1},{4,6},{5,7},{6,4},{7,5},{8,10},{9,11},{10,... | collective-permute-start | bytes 2555912 | tf_op jit(solution)/shard_map/ppermute | solution.py:821
  194.4 22.6 %collective-permute-start.23 = (bf16[4,16,2560]{2,1,0:T(8,128)(2,1)S(1)}, bf16[4,16,2560]{2,1,0:T(8,128)(2,1)S(1)}, u32[]{:S(2)}, u32[]{:S(2)}) collective-permute-start(bf16[4,16,2560]{2,1,0:T(8,128)(2,1)S(1)} %get-tuple-element.136), channel_id=1, source_target_pairs={{0,4},{1,5},{2,6},{3,7},{4,0},{5,1},{6,2},{7,3},{8,12},{9,13},{10,... | collective-permute-start | bytes 983048 | tf_op jit(solution)/shard_map/ppermute | solution.py:821
  196.3 20.7 %collective-permute-start.24 = (bf16[4,16,2560]{2,1,0:T(8,128)(2,1)S(1)}, bf16[4,16,2560]{2,1,0:T(8,128)(2,1)S(1)}, u32[]{:S(2)}, u32[]{:S(2)}) collective-permute-start(bf16[4,16,2560]{2,1,0:T(8,128)(2,1)S(1)} %get-tuple-element.137), channel_id=1, source_target_pairs={{0,5},{1,4},{2,7},{3,6},{4,1},{5,0},{6,3},{7,2},{8,13},{9,12},{10,... | collective-permute-start | bytes 983048 | tf_op jit(solution)/shard_map/ppermute | solution.py:821
  197.7 1.2 copy-start
  203.4 5.9 %copy-start.6 = (f32[3,16,128]{2,1,0:T(8,128)S(1)}, f32[3,16,128]{2,1,0:T(8,128)}, u32[]{:S(2)}) copy-start(f32[3,16,128]{2,1,0:T(8,128)} %get-tuple-element.165) | copy-start | bytes 73732
  203.5 5.9 %copy-start.7 = (f32[3,16,128]{2,1,0:T(8,128)S(1)}, f32[3,16,128]{2,1,0:T(8,128)}, u32[]{:S(2)}) copy-start(f32[3,16,128]{2,1,0:T(8,128)} %get-tuple-element.164) | copy-start | bytes 73732
  203.5 5.9 %copy-start.8 = (f32[3,16,128]{2,1,0:T(8,128)S(1)}, f32[3,16,128]{2,1,0:T(8,128)}, u32[]{:S(2)}) copy-start(f32[3,16,128]{2,1,0:T(8,128)} %get-tuple-element.163) | copy-start | bytes 73732
  205.8 11.2 %collective-permute-start.20 = (bf16[4,16,1664]{2,1,0:T(8,128)(2,1)}, bf16[4,16,1664]{2,1,0:T(8,128)(2,1)S(1)}, u32[]{:S(2)}, u32[]{:S(2)}) collective-permute-start(bf16[4,16,1664]{2,1,0:T(8,128)(2,1)} %get-tuple-element.133), channel_id=1, source_target_pairs={{0,1},{1,0},{2,3},{3,2},{4,5},{5,4},{6,7},{7,6},{8,9},{9,8},{10,11... | collective-permute-start | bytes 638984 | tf_op jit(solution)/shard_map/ppermute | solution.py:821
  206.1 16.6 %collective-permute-start.21 = (bf16[4,16,1664]{2,1,0:T(8,128)(2,1)S(1)}, bf16[4,16,1664]{2,1,0:T(8,128)(2,1)S(1)}, u32[]{:S(2)}, u32[]{:S(2)}) collective-permute-start(bf16[4,16,1664]{2,1,0:T(8,128)(2,1)S(1)} %get-tuple-element.134), channel_id=1, source_target_pairs={{0,4},{1,5},{2,6},{3,7},{4,0},{5,1},{6,2},{7,3},{8,12},{9,13},{10,... | collective-permute-start | bytes 638984 | tf_op jit(solution)/shard_map/ppermute | solution.py:821
  208.0 14.8 %collective-permute-start.22 = (bf16[4,16,1664]{2,1,0:T(8,128)(2,1)S(1)}, bf16[4,16,1664]{2,1,0:T(8,128)(2,1)S(1)}, u32[]{:S(2)}, u32[]{:S(2)}) collective-permute-start(bf16[4,16,1664]{2,1,0:T(8,128)(2,1)S(1)} %get-tuple-element.135), channel_id=1, source_target_pairs={{0,5},{1,4},{2,7},{3,6},{4,1},{5,0},{6,3},{7,2},{8,13},{9,12},{10,... | collective-permute-start | bytes 638984 | tf_op jit(solution)/shard_map/ppermute | solution.py:821
  209.9 1.0 copy-start.1
  211.0 11.8 %copy-start.3 = (bf16[4,16,2560]{2,1,0:T(8,128)(2,1)S(1)}, bf16[4,16,2560]{2,1,0:T(8,128)(2,1)}, u32[]{:S(2)}) copy-start(bf16[4,16,2560]{2,1,0:T(8,128)(2,1)} %copy-done.2) | copy-start | bytes 983044
  225.2 16.5 %collective-permute-start.25 = (bf16[16,4224]{1,0:T(8,128)(2,1)S(1)}, bf16[16,4224]{1,0:T(8,128)(2,1)S(1)}, u32[]{:S(2)}, u32[]{:S(2)}) collective-permute-start(bf16[16,4224]{1,0:T(8,128)(2,1)S(1)} %get-tuple-element.143), channel_id=1, source_target_pairs={{0,8},{1,9},{2,10},{3,11},{4,12},{5,13},{6,14},{7,15},{8,0},{9,1},... | collective-permute-start | bytes 405512 | tf_op jit(solution)/shard_map/ppermute | solution.py:821
  226.7 15.0 %collective-permute-start.26 = (bf16[16,4224]{1,0:T(8,128)(2,1)S(1)}, bf16[16,4224]{1,0:T(8,128)(2,1)S(1)}, u32[]{:S(2)}, u32[]{:S(2)}) collective-permute-start(bf16[16,4224]{1,0:T(8,128)(2,1)S(1)} %get-tuple-element.144), channel_id=1, source_target_pairs={{0,16},{1,17},{2,18},{3,19},{4,20},{5,21},{6,22},{7,23},{8,24},{9,... | collective-permute-start | bytes 405512 | tf_op jit(solution)/shard_map/ppermute | solution.py:821
  229.2 12.6 %collective-permute-start.27 = (bf16[16,4224]{1,0:T(8,128)(2,1)S(1)}, bf16[16,4224]{1,0:T(8,128)(2,1)S(1)}, u32[]{:S(2)}, u32[]{:S(2)}) collective-permute-start(bf16[16,4224]{1,0:T(8,128)(2,1)S(1)} %get-tuple-element.145), channel_id=1, source_target_pairs={{0,24},{1,25},{2,26},{3,27},{4,28},{5,29},{6,30},{7,31},{8,16},{9,... | collective-permute-start | bytes 405512 | tf_op jit(solution)/shard_map/ppermute | solution.py:821
  229.6 10.1 %copy-start.11 = (f32[3,8,128]{2,1,0:T(8,128)S(1)}, f32[3,8,128]{2,1,0:T(8,128)}, u32[]{:S(2)}) copy-start(f32[3,8,128]{2,1,0:T(8,128)} %get-tuple-element.160) | copy-start | bytes 36868
  229.6 10.1 %copy-start.5 = (s32[12,128]{1,0:T(8,128)S(1)}, s32[12,128]{1,0:T(8,128)}, u32[]{:S(2)}) copy-start(s32[12,128]{1,0:T(8,128)} %refs_4_.7) | copy-start | bytes 18436
  229.7 14.5 %copy-start.9 = (s32[12,256]{1,0:T(8,128)S(1)}, s32[12,256]{1,0:T(8,128)}, u32[]{:S(2)}) copy-start(s32[12,256]{1,0:T(8,128)} %refs_2_.7) | copy-start | bytes 36868
  239.9 0.9 copy-start.4
  244.2 11.8 %all-to-all-start = ((f32[32,1,128]{2,1,0:T(1,128)}), f32[32,1,128]{2,1,0:T(1,128)S(1)}, u32[]{:S(2)}, u32[]{:S(2)}) async-start(f32[32,1,128]{2,1,0:T(1,128)} %bitcast.22), calls=%async_computation.2 | async-start | bytes 32768 | tf_op jit(solution)/shard_map/all_to_all | solution.py:924
Sparse Core Ops, SparseCore 0:
  11.6 69.4 all-gather.2
  140.0 12.2 reduce-scatter.5
  164.8 45.0 reduce-scatter.9
  212.0 23.2 reduce-scatter.7
where the time goes:
time: 267 us; the launch traced here: 265 us
  Pallas kernels  171 us (64%)
  waiting for transfers between devices  37.8 us (14%)
  starting transfers between devices  30.9 us (12%)
  between operations  16.1 us (6%)
  local copies, waits for them, and re-layouts  7.2 us (3%)
    pallas_call x10, Pallas kernels, call(): pl.pallas_call(kernel, out_shape=outs, grid_spec=pltpu.PrefetchScalarGrid...  159 us
    ppermute x28, waiting for transfers between devices, shift(): return lax.ppermute(array, FINE, [(i, i ^ mask) for i in range(32)])  31.3 us
    ppermute x28, starting transfers between devices, shift(): return lax.ppermute(array, FINE, [(i, i ^ mask) for i in range(32)])  26.2 us
    pallas_call x5, Pallas kernels, small_call(): pl.pallas_call(ignoring(staged(kernel, len(ins), len(outs)), len(ins), le...  8.03 us
    all_to_all x1, waiting for transfers between devices, on_device(): sent = lax.all_to_all(square, FINE, 0, 0, tiled=True)  6 us
    unnamed x27, local copies, waits for them, and re-layouts  5.74 us
  transfers between devices with their start and end apart: 33, of which 14 were waited for; matrix products, arithmetic and copies ran while one was open for 1% of the time, Pallas kernels for 45%

commit v1 on v0

--- a/solution.py
+++ b/solution.py
@@ -70,6 +70,12 @@
     return copies
 
 
+def column_pairs(me_ref, pieces, weight_ref):
+    return [
+        (piece, weight_ref.at[:, (me_ref[0] ^ CODES[4 * t]) & 7]) for t, piece in enumerate(pieces)
+    ]
+
+
 def read_rows(grad_w, block):
     return grad_w[block_rows(block), :].astype(BF16)
 
@@ -130,23 +136,18 @@
 def self_forward_kernel(me_ref, tokens_ref, dec_ref, padding_ref, buckets_ref, *refs):
     pieces, refs = refs[:8], refs[8:]
     input_ref, qkv_ref, prob_ref, attended_ref, weight_ref, gains_ref = refs[:6]
-    bias_ref, small_ref, sems = refs[6:]
+    bias_ref, sems = refs[6:]
     length = dec_ref.shape[1]
     width = tokens_ref.shape[1]
 
     @pl.when(pl.program_id(0) == 0)
     def _():
-        pairs = []
-        for k, code in enumerate(CODES):
-            rows = block_rows(me_ref[0] ^ code)
-            source = pieces[k // 4].at[k % 4]
-            pairs.append((source.at[:, : 3 * width], weight_ref.at[rows, :]))
-            pairs.append((source.at[:, 3 * width :], small_ref.at[rows, :]))
-        for copy in start_copies(pairs, sems):
+        for copy in start_copies(column_pairs(me_ref, pieces, weight_ref), sems):
             copy.wait()
+        small_lines = weight_ref[:, :, :, 3 * width :].reshape(width, LANES)
         first = lax.broadcasted_iota(jnp.int32, (32, width), 1)
         pick = first == 16 * lax.broadcasted_iota(jnp.int32, (32, width), 0)
-        small = nn(pick.astype(F32).astype(BF16), small_ref[...]).astype(BF16)
+        small = nn(pick.astype(F32).astype(BF16), small_lines).astype(BF16)
         lane = lax.broadcasted_iota(jnp.int32, (LANES, width), 0)
         feature = lax.broadcasted_iota(jnp.int32, (LANES, width), 1)
         block = lax.broadcasted_iota(jnp.int32, (32, width), 0)
@@ -172,7 +173,9 @@
     input_ref[...] = normed
     for first in range(0, 3 * width, 256):
         cols = slice(first, first + 256)
-        qkv_ref[:, cols] = nn(normed, weight_ref[:, cols]).astype(BF16)
+        qkv_ref[:, cols] = nn(
+            normed, weight_ref[:, :, :, cols].reshape(width, 256)
+        ).astype(BF16)
 
     step = pl.program_id(0)
     count = tokens_ref.shape[0] // length
@@ -210,34 +213,29 @@
     pipelined(row_pairs(count), scores, weigh, mix)
 
 
-def memory_forward_kernel(me_ref, memory_ref, *refs):
-    pieces, (kv_ref, weight_ref, sems) = refs[:-3], refs[-3:]
-    width = memory_ref.shape[1]
+def cross_forward_kernel(me_ref, tokens_ref, attended_a_ref, memory_ref, dec_ref, mem_ref,
+                         gains_ref, *refs):
+    pieces, refs = refs[:8], refs[8:]
+    (middle_ref, input_ref, query_ref, kv_ref, prob_ref, attended_ref, after_ref, weight_ref,
+     sems) = refs
+    mem_length, length = mem_ref.shape[1], dec_ref.shape[1]
+    width = tokens_ref.shape[1]
 
     @pl.when(pl.program_id(0) == 0)
     def _():
-        pairs = []
-        for k, code in enumerate(CODES):
-            source = pieces[k // 4].at[k % 4]
-            pairs.append((source, weight_ref.at[block_rows(me_ref[0] ^ code), :]))
-        for copy in start_copies(pairs, sems):
+        for copy in start_copies(column_pairs(me_ref, pieces, weight_ref), sems):
             copy.wait()
 
-    for first in range(0, 2 * width, 256):
-        kv_ref[:, first : first + 256] = nn(
-            memory_ref[...], weight_ref[:, 2 * width + first : 2 * width + first + 256]
-        ).astype(BF16)
-
-
-def cross_forward_kernel(tokens_ref, attended_a_ref, kv_ref, dec_ref, mem_ref, gains_ref,
-                         weight_ref, middle_ref, input_ref, query_ref, prob_ref, attended_ref, after_ref):
-    mem_length, length = mem_ref.shape[1], dec_ref.shape[1]
-    width = tokens_ref.shape[1]
-    values = tokens_ref[...].astype(F32) + nn(attended_a_ref[...], weight_ref[:, :width])
+    def weight(k):
+        return weight_ref[:, :, :, k * width : (k + 1) * width].reshape(width, width)
+
+    for k in range(2):
+        kv_ref[:, k * width : (k + 1) * width] = nn(memory_ref[...], weight(k + 2)).astype(BF16)
+    values = tokens_ref[...].astype(F32) + nn(attended_a_ref[...], weight(0))
     middle_ref[...] = values.astype(BF16)
     normed = (values * inverse_root(values) * gains_ref[1:2, :]).astype(BF16)
     input_ref[...] = normed
-    query_ref[...] = nn(normed, weight_ref[:, width : 2 * width]).astype(BF16)
+    query_ref[...] = nn(normed, weight(1)).astype(BF16)
 
     step = pl.program_id(0)
     count = tokens_ref.shape[0] // length
@@ -272,7 +270,7 @@
         attended_ref[rows, lanes] = fold_pair(nn(value, prob), length)
 
     pipelined(row_pairs(count), scores, weigh, mix)
-    after = values + nn(attended_ref[...], weight_ref[:, 4 * width :])
+    after = values + nn(attended_ref[...], weight(4))
     after_ref[...] = after.astype(BF16)
 
 
@@ -544,7 +542,7 @@
     step = pl.program_id(0)
     width = tokens_ref.shape[1]
     grad_qkv = grad_qkv_ref[...]
-    grad_normed = nt(grad_qkv, weight_ref[...])
+    grad_normed = nt(grad_qkv, weight_ref[:, : 3 * width])
     grad, terms = norm_back(tokens_ref[...].astype(F32), gains_ref[0:1, :], grad_normed)
     grad_tokens_ref[...] = (branch_ref[...].astype(F32) + grad).astype(BF16)
 
@@ -684,27 +682,32 @@
     )(*ins, *after)
 
 
-def split_kernel(*refs):
-    lines, (own_ref, rest_ref) = refs[:4], refs[4:]
-    split = own_ref.shape[2]
-    for s, line in enumerate(lines):
-        own_ref[s] = line[:, :split]
-        rest_ref[s] = line[:, split:]
-
-
-def split_column(lines, split):
-    rows, cols = lines[0].shape
-    outs = [shape_of((4, rows, part), BF16) for part in (split, cols - split)]
-    return small_call(split_kernel, lines, (), outs)
+def stack_kernel(me_ref, *refs):
+    lines, out_ref, sems = refs[:-2], refs[-2], refs[-1]
+    pairs = [(line, out_ref.at[me_ref[0] ^ s]) for s, line in enumerate(lines)]
+    for copy in start_copies(pairs, sems):
+        copy.wait()
+
+
+def stack_lines(place, lines):
+    return pl.pallas_call(
+        stack_kernel,
+        out_shape=shape_of((len(lines),) + lines[0].shape, BF16),
+        in_specs=[pl.BlockSpec(memory_space=pltpu.SMEM)]
+        + [pl.BlockSpec(memory_space=pl.ANY)] * len(lines),
+        out_specs=pl.BlockSpec(memory_space=pl.ANY),
+        scratch_shapes=[pltpu.SemaphoreType.DMA((len(lines),))],
+        compiler_params=pltpu.CompilerParams(vmem_limit_bytes=SHARED_LIMIT),
+    )(jnp.full((1,), place, jnp.int32), *lines)
 
 
 def pack_kernel(*refs):
-    ins, (shard_ref, feed_ref) = refs[:11], refs[11:]
+    ins, (own_ref, cross_ref, feed_ref) = refs[:11], refs[11:]
     width = ins[0].shape[1]
-    start = 0
-    for line in (*ins[:3], ins[10], *ins[3:8]):
-        shard_ref[:, start : start + line.shape[1]] = line[...]
-        start += line.shape[1]
+    for k, line in enumerate((*ins[:3], ins[10])):
+        own_ref[:, k * width : k * width + line.shape[1]] = line[...]
+    for k in range(5):
+        cross_ref[:, k * width : (k + 1) * width] = ins[3 + k][...]
     for j in range(ins[8].shape[1] // width):
         feed_ref[16 * j : 16 * (j + 1), :] = ins[8][:, j * width : (j + 1) * width]
     feed_ref[64:, :] = ins[9][...]
@@ -712,7 +715,8 @@
 
 def pack(weights, small):
     width = weights[0].shape[1]
-    outs = [shape_of((16, 8 * width + LANES), BF16), shape_of((128, width), BF16)]
+    outs = [shape_of((16, cols), BF16) for cols in (3 * width + LANES, 5 * width)]
+    outs.append(shape_of((128, width), BF16))
     return small_call(pack_kernel, (*map(in_hbm, weights), small), (), outs)
 
 
@@ -866,13 +870,18 @@
     def __init__(self, weights):
         self.me = lax.axis_index(FINE)
         small = small_row(weights[10:13], weights[13])
-        shard, feed = pack(weights[:10], small)
+        own, rest, feed = pack(weights[:10], small)
         self.feed = lax.all_gather(feed, FINE, axis=0)
-        column = [shard, *shift_column([shard] * 3)]
-        own, rest = split_column(column, 3 * weights[0].shape[1] + LANES)
+        z = self.me >> 3
+        own = stack_lines(z, [own, *shift_column([own] * 3)])
+        rest = hold(rest, own)
+        pair = stack_lines(z & 1, [rest, shift(rest, COLUMN[1])])
+        other = shift(pair, COLUMN[2])
+        rest = stack_lines(z >> 1, [pair, other]).reshape((4,) + rest.shape)
         plane = [own, *shift_plane([own] * 3)]
+        self.own = plane + [shift(hold(piece, other), 2) for piece in plane]
+        rest = hold(rest, plane[1])
         self.plane = [rest, *shift_plane([rest] * 3)]
-        self.own = plane + [shift(piece, 2) for piece in plane]
 
     def cross(self, after):
         plane = [hold(piece, after) for piece in self.plane]
@@ -955,28 +964,27 @@
             kept((seqs, PAIRS, length, 2 * length), BF16),
             kept((dec, width), BF16),
         ),
-        (kept((width, 3 * width), BF16), kept((8, width), F32)),
-        [pltpu.VMEM((PAIRS, length, 2 * length), F32), pltpu.VMEM((width, LANES), BF16), dma((64,))],
+        (kept((4, 8, 16, 3 * width + LANES), BF16), kept((8, width), F32)),
+        [pltpu.VMEM((PAIRS, length, 2 * length), F32), dma((8,))],
         6 * flops, ("iwww", "iiiiww"), (), SHARED_LIMIT,
     )
-    kv_b, cross_w = call(
-        memory_forward_kernel, small_steps, me, (memory2,), (), way.cross(attended_a),
-        (kept((mem, 2 * width), BF16),), (kept((width, 5 * width), BF16),), [dma((32,))],
-        4 * flops, ("i", "iw"), (), SHARED_LIMIT,
-    )
-    middle, input_b, query_b, prob_b, attended_b, after_cross = call(
-        cross_forward_kernel, small_steps, None, (tokens2, attended_a, kv_b),
-        (dec_segments, mem_segments, gains, cross_w), (),
+    middle, input_b, query_b, kv_b, prob_b, attended_b, after_cross, cross_w = call(
+        cross_forward_kernel, steps, me, (tokens2, attended_a, memory2),
+        (dec_segments, mem_segments, gains), way.cross(attended_a),
         (
             kept((dec, width), BF16),
             kept((dec, width), BF16),
             kept((dec, width), BF16),
+            kept((mem, 2 * width), BF16),
             kept((seqs, PAIRS, mem_length, 2 * length), BF16),
             kept((dec, width), BF16),
             kept((dec, width), BF16),
         ),
-        (), [], 6 * flops, ("iiiwwww", "iiiiii"),
+        (kept((4, 8, 16, 5 * width), BF16),),
+        [dma((8,))],
+        10 * flops, ("iiiwww", "iiiiiiiw"), (), SHARED_LIMIT,
     )
+    self_w, cross_w = self_w.reshape(width, -1), cross_w.reshape(width, -1)
     total, square = kept((1, width), F32), shape_of((steps, 4 * STEP_ROWS, LANES), F32)
     token_shape = shape_of((steps, 8, length), F32)
     small_token = shape_of((small_steps, 8, length), F32)

time: 267 us -> 256 us (0.959)
  Pallas kernels: 171 us -> 163 us
  waiting for transfers between devices: 37.8 us -> 34 us
    pallas_call x10 -> x9, Pallas kernels: 159 us -> 151 us  [call(): pl.pallas_call(kernel, out_shape=outs, grid_spec=pltpu.PrefetchScalarGrid...]
    ppermute x28 -> x30, waiting for transfers between devices: 31.3 us -> 27.7 us  [shift(): return lax.ppermute(array, FINE, [(i, i ^ mask) for i in range(32)])]
    ppermute x28 -> x30, starting transfers between devices: 26.2 us -> 29.3 us  [shift(): return lax.ppermute(array, FINE, [(i, i ^ mask) for i in range(32)])]
    pallas_call x5 -> x4, Pallas kernels: 8.03 us -> 6.9 us  [small_call(): pl.pallas_call(ignoring(staged(kernel, len(ins), len(outs)), len(ins), le...]
  transfers between devices with their start and end apart: 33 -> 35, of which waited for: 14 -> 13; matrix products, arithmetic and copies ran while one was open for 1% -> 1% of each run, Pallas kernels for 45% -> 43%
where the time goes in v1:
time: 256 us; the launch traced here: 254 us
  Pallas kernels  163 us (64%)
  waiting for transfers between devices  34 us (13%)
  starting transfers between devices  32.7 us (13%)
  between operations  16.1 us (6%)
  local copies, waits for them, and re-layouts  7.18 us (3%)
    pallas_call x9, Pallas kernels, call(): pl.pallas_call(kernel, out_shape=outs, grid_spec=pltpu.PrefetchScalarGrid...  151 us
    ppermute x30, starting transfers between devices, shift(): return lax.ppermute(array, FINE, [(i, i ^ mask) for i in range(32)])  29.3 us
    ppermute x30, waiting for transfers between devices, shift(): return lax.ppermute(array, FINE, [(i, i ^ mask) for i in range(32)])  27.7 us
    pallas_call x4, Pallas kernels, small_call(): pl.pallas_call(ignoring(staged(kernel, len(ins), len(outs)), len(ins), le...  6.9 us
    all_to_all x1, waiting for transfers between devices, on_device(): sent = lax.all_to_all(square, FINE, 0, 0, tiled=True)  6 us
    unnamed x27, local copies, waits for them, and re-layouts  5.71 us
  transfers between devices with their start and end apart: 35, of which 13 were waited for; matrix products, arithmetic and copies ran while one was open for 1% of the time, Pallas kernels for 43%

profile of v1, /device:TPU:0, one launch (start us, length us, event | category | flops | bytes accessed | tf_op | source)
XLA Modules:
  0.0 254.4 jit_solution(17747102929785200522)
XLA Ops:
  7.2 0.8 fusion.2
  8.0 2.0 shard_map.348
  10.1 5.1 %collective-permute-start.2 = (bf16[16,1664]{1,0:T(8,128)(2,1)S(1)}, bf16[16,1664]{1,0:T(8,128)(2,1)S(1)}, u32[]{:S(2)}, u32[]{:S(2)}) collective-permute-start(bf16[16,1664]{1,0:T(8,128)(2,1)S(1)} %get-tuple-element.98.refs_0_), channel_id=1, source_target_pairs={{0,24},{1,25},{2,26},{3,27},{4,28},{5,29},{6,30},{7,31},{8,16},{9,... | collective-permute-start | bytes 159752 | tf_op jit(solution)/shard_map/ppermute | solution.py:825
  15.2 0.6 collective-permute-start
  15.9 1.7 collective-permute-done.2.refs_3_
  17.5 2.7 %collective-permute-done.1.refs_2_ = bf16[16,1664]{1,0:T(8,128)(2,1)S(1)} collective-permute-done((bf16[16,1664]{1,0:T(8,128)(2,1)S(1)}, bf16[16,1664]{1,0:T(8,128)(2,1)S(1)}, u32[]{:S(2)}, u32[]{:S(2)}) %collective-permute-start.1) | collective-permute-done | bytes 53280 | tf_op jit(solution)/shard_map/ppermute | solution.py:825
  20.6 0.9 collective-permute-start.6
  21.5 2.4 collective-permute-start.5
  25.3 2.1 collective-permute-start.7
  27.4 9.0 %collective-permute-done.7.refs_1_ = bf16[2,16,2560]{2,1,0:T(8,128)(2,1)S(1)} collective-permute-done((bf16[2,16,2560]{2,1,0:T(8,128)(2,1)S(1)}, bf16[2,16,2560]{2,1,0:T(8,128)(2,1)S(1)}, u32[]{:S(2)}, u32[]{:S(2)}) %collective-permute-start.7) | collective-permute-done | bytes 163872 | tf_op jit(solution)/shard_map/ppermute | solution.py:825
  37.8 2.5 collective-permute-start.14
  40.7 0.6 collective-permute-start.12
  41.4 10.3 %shard_map.351 = (bf16[1536,512]{1,0:T(8,128)(2,1)}, bf16[1536,1536]{1,0:T(8,128)(2,1)}, bf16[12,4,128,256]{3,2,1,0:T(8,128)(2,1)}, bf16[1536,512]{1,0:T(8,128)(...) custom-call(s32[1]{0:T(128)} %bitcast.refs_0_, bf16[1536,512]{1,0:T(8,128)(2,1)} %bitcast.56, ...), custom_call_target="tpu_custom_call" | custom-call | flops 4831838208 | bytes 16019968 | tf_op jit(solution)/shard_map/pallas_call | solution.py:796
  51.7 1.3 collective-permute-done.14.refs_10_
  53.1 4.3 %collective-permute-done.13.refs_9_ = bf16[4,16,2560]{2,1,0:T(8,128)(2,1)S(1)} collective-permute-done((bf16[4,16,2560]{2,1,0:T(8,128)(2,1)S(1)}, bf16[4,16,2560]{2,1,0:T(8,128)(2,1)S(1)}, u32[]{:S(2)}, u32[]{:S(2)}) %collective-permute-start.13) | collective-permute-done | bytes 327712 | tf_op jit(solution)/shard_map/ppermute | solution.py:825
  57.4 1.9 collective-permute-done.12.refs_8_
  59.8 1.1 collective-permute-done.16.refs_12_
  61.8 20.6 %shard_map.353 = (bf16[1536,512]{1,0:T(8,128)(2,1)}, bf16[1536,512]{1,0:T(8,128)(2,1)}, bf16[1536,512]{1,0:T(8,128)(2,1)}, bf16[3072,1024]{1,0:T(8,128)(2,1)}, b...) custom-call(s32[1]{0:T(128)} %bitcast.refs_0_, ...), custom_call_target="tpu_custom_call" | custom-call | flops 8053063680 | bytes 32016384 | tf_op jit(solution)/shard_map/pallas_call | solution.py:796
  82.6 48.7 %shard_map.354 = (bf16[1536,512]{1,0:T(8,128)(2,1)}, bf16[1536,512]{1,0:T(8,128)(2,1)}, bf16[32,128,512]{2,1,0:T(8,128)(2,1)}, f32[1,512]{1,0:T(1,128)}, f32[3,16,128]{2,1,0:T(8,128)}, /*index=5*/f32[3,8,128]{2,1,0:T(8,128)}) custom-call(bf16[1536,512]{1,0:T(8,128)(2,1)} %get-tuple-element.112.refs_0_, bf16[1536,512]{1,0:T(8,128)(2,1)} %bitcast.55, ...), custom_call_target="tpu_custom_call" | custom-call | flops 20937965568 | bytes 14747648 | tf_op jit(solution)/shard_map/pallas_call | solution.py:796
  131.4 25.4 %shard_map.355 = (bf16[1536,512]{1,0:T(8,128)(2,1)}, bf16[3072,1024]{1,0:T(8,128)(2,1)}, bf16[1536,512]{1,0:T(8,128)(2,1)}, bf16[16,16,2560]{2,1,0:T(8,128)(2,1)...) custom-call(s32[1]{0:T(128)} %bitcast.refs_0_, ...), custom_call_target="tpu_custom_call" | custom-call | flops 16106127360 | bytes 39895040 | tf_op jit(solution)/shard_map/pallas_call | solution.py:796
  156.9 1.2 copy-done.12
  158.3 13.5 %shard_map.356 = (bf16[1536,1536]{1,0:T(8,128)(2,1)}, f32[8,128]{1,0:T(8,128)}, f32[3,4,8,128]{3,2,1,0:T(8,128)}) custom-call(bf16[1536,512]{1,0:T(8,128)(2,1)} %get-tuple-element.123.refs_0_.refs_1_.refs_3_, bf16[1536,1536]{1,0:T(8,128)(2,1)} %get-tuple-element.125.refs_1_, bf16[12,4,128,256]{3,2,1,0:T(8,128)(2,1)} %get-tuple-element.126.refs_2_, ...), custom_call_target="tpu_custom_call" | custom-call | flops 8053063680 | bytes 16837120 | tf_op jit(solution)/shard_map/pallas_call | solution.py:796
  171.9 1.8 shard_map.357
  173.7 0.7 copy-done.2
  174.4 0.8 collective-permute-start.20
  175.2 11.8 %shard_map.358 = (bf16[1536,512]{1,0:T(8,128)(2,1)}, bf16[16,16,1664]{2,1,0:T(8,128)(2,1)}, bf16[16,16,1664]{2,1,0:T(8,128)(2,1)}, f32[3,16,128]{2,1,0:T(8,128)}) custom-call(s32[1]{0:T(128)} %bitcast.refs_0_, bf16[1536,512]{1,0:T(8,128)(2,1)} %get-tuple-element.123.refs_0_.refs_1_.refs_3_, bf16[1536,512]{1,0:T(8,128)(2,1)} %bitcast.58, ...), custom_call_target="tpu_custom_call" | custom-call | flops 5637144576 | bytes 14800896 | tf_op jit(solution)/shard_map/pallas_call | solution.py:796
  187.2 0.7 collective-permute-start.25
  187.8 2.1 collective-permute-start.26
  190.0 1.2 copy-done
  191.1 4.5 %shard_map.359.refs_2_ = f32[3,8,128]{2,1,0:T(8,128)S(1)} custom-call(bf16[1536,512]{1,0:T(8,128)(2,1)} %get-tuple-element.117.refs_5_.refs_0_, bf16[1536,512]{1,0:T(8,128)(2,1)} %get-tuple-element.141.refs_1_, bf16[1536,512]{1,0:T(8,128)(2,1)} %get-tuple-element.121.refs_9_.refs_2_, bf16[1536,512]{1,0:T(8,128)(2,1)} %get-tuple-element.115.refs_1_.refs_3_, ...), custom_call_target="tpu_custom_call" | custom-call | flops 1610612736 | bytes 7161856 | tf_op jit(solution)/shard_map/pallas_call | solution.py:796
  195.7 2.3 shard_map.360
  198.0 0.8 collective-permute-start.22
  199.4 2.1 collective-permute-start.24
  201.8 1.0 copy-done.1
  202.8 6.0 %shard_map.361.refs_8_ = f32[3,8,128]{2,1,0:T(8,128)S(1)} custom-call(bf16[1536,512]{1,0:T(8,128)(2,1)} %get-tuple-element.124.refs_3_.refs_0_, bf16[1536,1536]{1,0:T(8,128)(2,1)} %get-tuple-element.127.refs_2_.refs_4_.refs_1_, bf16[1536,512]{1,0:T(8,128)(2,1)} %get-tuple-element.105.refs_2_.refs_4_, ...), custom_call_target="tpu_custom_call" | custom-call | flops 1610612736 | bytes 10192896 | tf_op jit(solution)/shard_map/pallas_call | solution.py:796
  208.9 4.6 %collective-permute-done.23.refs_2_ = bf16[4,16,1664]{2,1,0:T(8,128)(2,1)S(1)} collective-permute-done((bf16[4,16,1664]{2,1,0:T(8,128)(2,1)S(1)}, bf16[4,16,1664]{2,1,0:T(8,128)(2,1)S(1)}, u32[]{:S(2)}, u32[]{:S(2)}) %collective-permute-start.23) | collective-permute-done | bytes 213024 | tf_op jit(solution)/shard_map/ppermute | solution.py:825
  213.5 2.4 shard_map.362
  215.9 1.4 collective-permute-start.27
  217.3 1.1 collective-permute-start.28
  218.4 1.9 collective-permute-start.29
  220.4 10.1 %shard_map.363 = (bf16[3072,512]{1,0:T(8,128)(2,1)}, f32[3,8,256]{2,1,0:T(8,128)S(1)}) custom-call(bf16[3072,512]{1,0:T(8,128)(2,1)} %bitcast.54, bf16[3072,1024]{1,0:T(8,128)(2,1)} %get-tuple-element.136.refs_1_, s32[12,256]{1,0:T(8,128)} %refs_2_.7, bf16[512,2560]{1,0:T(8,128)(2,1)} %bitcast.64, f32[16,4224]{1,0:T(8,128)S(1)} %get-tuple-element.151.refs_4_.refs_0_), custom_call_target="tpu_custom_call" | custom-call | flops 8053063680 | bytes 15511552 | tf_op jit(solution)/shard_map/pallas_call | solution.py:796
  230.6 0.9 copy-done.4
  231.5 0.9 shard_map.364
  232.4 1.6 shard_map.365
  234.1 0.7 slice_reduce_fusion.2
  234.9 3.2 %all-to-all-start = ((f32[32,1,128]{2,1,0:T(1,128)}), f32[32,1,128]{2,1,0:T(1,128)S(1)}, u32[]{:S(2)}, u32[]{:S(2)}) async-start(f32[32,1,128]{2,1,0:T(1,128)} %bitcast.28), calls=%async_computation.2 | async-start | bytes 32768 | tf_op jit(solution)/shard_map/all_to_all | solution.py:933
  238.7 0.7 copy.53
  239.3 6.0 %all-to-all-done = f32[32,1,128]{2,1,0:T(1,128)S(1)} async-done(((f32[32,1,128]{2,1,0:T(1,128)}), f32[32,1,128]{2,1,0:T(1,128)S(1)}, u32[]{:S(2)}, u32[]{:S(2)}) %all-to-all-start) | async-done | bytes 16416 | tf_op jit(solution)/shard_map/all_to_all | solution.py:933
  (88 shorter events, 8.2 us)
Async XLA Ops:
  7.2 75.4 %all-gather.3.cloned.1.call-start = ((), (), s32[]{:S(2)}) async-start(), calls=%async_computation.6 | async-start | bytes 4325376 | tf_op jit(solution)/shard_map/all_gather | solution.py:874
  10.1 146.8 %reduce-scatter.6.cloned.1.call-start = ((), (), s32[]{:S(2)}) async-start(), calls=%async_computation.4 | async-start | bytes 6291456 | tf_op jit(solution)/shard_map/reduce_scatter | solution.py:891
  10.1 7.4 %collective-permute-start.2 = (bf16[16,1664]{1,0:T(8,128)(2,1)S(1)}, bf16[16,1664]{1,0:T(8,128)(2,1)S(1)}, u32[]{:S(2)}, u32[]{:S(2)}) collective-permute-start(bf16[16,1664]{1,0:T(8,128)(2,1)S(1)} %get-tuple-element.98.refs_0_), channel_id=1, source_target_pairs={{0,24},{1,25},{2,26},{3,27},{4,28},{5,29},{6,30},{7,31},{8,16},{9,... | collective-permute-start | bytes 159752 | tf_op jit(solution)/shard_map/ppermute | solution.py:825
  15.2 5.0 %collective-permute-start.1 = (bf16[16,1664]{1,0:T(8,128)(2,1)S(1)}, bf16[16,1664]{1,0:T(8,128)(2,1)S(1)}, u32[]{:S(2)}, u32[]{:S(2)}) collective-permute-start(bf16[16,1664]{1,0:T(8,128)(2,1)S(1)} %get-tuple-element.98.refs_0_), channel_id=1, source_target_pairs={{0,16},{1,17},{2,18},{3,19},{4,20},{5,21},{6,22},{7,23},{8,24},{9,... | collective-permute-start | bytes 159752 | tf_op jit(solution)/shard_map/ppermute | solution.py:825
  15.2 5.0 %collective-permute-start = (bf16[16,1664]{1,0:T(8,128)(2,1)S(1)}, bf16[16,1664]{1,0:T(8,128)(2,1)S(1)}, u32[]{:S(2)}, u32[]{:S(2)}) collective-permute-start(bf16[16,1664]{1,0:T(8,128)(2,1)S(1)} %get-tuple-element.98.refs_0_), channel_id=1, source_target_pairs={{0,8},{1,9},{2,10},{3,11},{4,12},{5,13},{6,14},{7,15},{8,0},{9,1},... | collective-permute-start | bytes 159752 | tf_op jit(solution)/shard_map/ppermute | solution.py:825
  20.6 4.5 %collective-permute-start.6 = (bf16[16,2560]{1,0:T(8,128)(2,1)S(1)}, bf16[16,2560]{1,0:T(8,128)(2,1)S(1)}, u32[]{:S(2)}, u32[]{:S(2)}) collective-permute-start(bf16[16,2560]{1,0:T(8,128)(2,1)S(1)} %get-tuple-element.100.refs_0_), channel_id=1, source_target_pairs={{0,8},{1,9},{2,10},{3,11},{4,12},{5,13},{6,14},{7,15},{8,0},{9,1},... | collective-permute-start | bytes 245768 | tf_op jit(solution)/shard_map/ppermute | solution.py:825
  21.5 14.9 %collective-permute-start.5 = (bf16[4,16,1664]{2,1,0:T(8,128)(2,1)S(1)}, bf16[4,16,1664]{2,1,0:T(8,128)(2,1)S(1)}, u32[]{:S(2)}, u32[]{:S(2)}) collective-permute-start(bf16[4,16,1664]{2,1,0:T(8,128)(2,1)S(1)} %shard_map.349.refs_5_), channel_id=1, source_target_pairs={{0,5},{1,4},{2,7},{3,6},{4,1},{5,0},{6,3},{7,2},{8,13},{9,12},{10,... | collective-permute-start | bytes 638984 | tf_op jit(solution)/shard_map/ppermute | solution.py:825
  23.9 12.9 %collective-permute-start.4 = (bf16[4,16,1664]{2,1,0:T(8,128)(2,1)S(1)}, bf16[4,16,1664]{2,1,0:T(8,128)(2,1)S(1)}, u32[]{:S(2)}, u32[]{:S(2)}) collective-permute-start(bf16[4,16,1664]{2,1,0:T(8,128)(2,1)S(1)} %shard_map.349.refs_5_), channel_id=1, source_target_pairs={{0,4},{1,5},{2,6},{3,7},{4,0},{5,1},{6,2},{7,3},{8,12},{9,13},{10,... | collective-permute-start | bytes 638984 | tf_op jit(solution)/shard_map/ppermute | solution.py:825
  24.4 12.5 %collective-permute-start.3 = (bf16[4,16,1664]{2,1,0:T(8,128)(2,1)S(1)}, bf16[4,16,1664]{2,1,0:T(8,128)(2,1)S(1)}, u32[]{:S(2)}, u32[]{:S(2)}) collective-permute-start(bf16[4,16,1664]{2,1,0:T(8,128)(2,1)S(1)} %shard_map.349.refs_5_), channel_id=1, source_target_pairs={{0,1},{1,0},{2,3},{3,2},{4,5},{5,4},{6,7},{7,6},{8,9},{9,8},{10,11... | collective-permute-start | bytes 638984 | tf_op jit(solution)/shard_map/ppermute | solution.py:825
  25.3 11.1 %collective-permute-start.7 = (bf16[2,16,2560]{2,1,0:T(8,128)(2,1)S(1)}, bf16[2,16,2560]{2,1,0:T(8,128)(2,1)S(1)}, u32[]{:S(2)}, u32[]{:S(2)}) collective-permute-start(bf16[2,16,2560]{2,1,0:T(8,128)(2,1)S(1)} %shard_map.350.refs_0_), channel_id=1, source_target_pairs={{0,16},{1,17},{2,18},{3,19},{4,20},{5,21},{6,22},{7,23},{8,24},{9,... | collective-permute-start | bytes 491528 | tf_op jit(solution)/shard_map/ppermute | solution.py:825
  36.3 4.0 %collective-permute-start.8 = (bf16[4,16,1664]{2,1,0:T(8,128)(2,1)S(1)}, bf16[4,16,1664]{2,1,0:T(8,128)(2,1)S(1)}, u32[]{:S(2)}, u32[]{:S(2)}) collective-permute-start(bf16[4,16,1664]{2,1,0:T(8,128)(2,1)S(1)} %shard_map.349.refs_5_), channel_id=1, source_target_pairs={{0,2},{1,3},{2,0},{3,1},{4,6},{5,7},{6,4},{7,5},{8,10},{9,11},{10,... | collective-permute-start | bytes 638984 | tf_op jit(solution)/shard_map/ppermute | solution.py:825
  36.4 4.4 %collective-permute-start.11 = (bf16[4,16,1664]{2,1,0:T(8,128)(2,1)S(1)}, bf16[4,16,1664]{2,1,0:T(8,128)(2,1)S(1)}, u32[]{:S(2)}, u32[]{:S(2)}) collective-permute-start(bf16[4,16,1664]{2,1,0:T(8,128)(2,1)S(1)} %collective-permute-done.5.refs_8_), channel_id=1, source_target_pairs={{0,2},{1,3},{2,0},{3,1},{4,6},{5,7},{6,4},{7,5},{8,10},{9,11},{10,... | collective-permute-start | bytes 638984 | tf_op jit(solution)/shard_map/ppermute | solution.py:825
  36.9 4.5 %collective-permute-start.10 = (bf16[4,16,1664]{2,1,0:T(8,128)(2,1)S(1)}, bf16[4,16,1664]{2,1,0:T(8,128)(2,1)S(1)}, u32[]{:S(2)}, u32[]{:S(2)}) collective-permute-start(bf16[4,16,1664]{2,1,0:T(8,128)(2,1)S(1)} %collective-permute-done.4.refs_7_), channel_id=1, source_target_pairs={{0,2},{1,3},{2,0},{3,1},{4,6},{5,7},{6,4},{7,5},{8,10},{9,11},{10,... | collective-permute-start | bytes 638984 | tf_op jit(solution)/shard_map/ppermute | solution.py:825
  36.9 4.4 %collective-permute-start.9 = (bf16[4,16,1664]{2,1,0:T(8,128)(2,1)S(1)}, bf16[4,16,1664]{2,1,0:T(8,128)(2,1)S(1)}, u32[]{:S(2)}, u32[]{:S(2)}) collective-permute-start(bf16[4,16,1664]{2,1,0:T(8,128)(2,1)S(1)} %collective-permute-done.3.refs_6_), channel_id=1, source_target_pairs={{0,2},{1,3},{2,0},{3,1},{4,6},{5,7},{6,4},{7,5},{8,10},{9,11},{10,... | collective-permute-start | bytes 638984 | tf_op jit(solution)/shard_map/ppermute | solution.py:825
  37.8 15.3 %collective-permute-start.14 = (bf16[4,16,2560]{2,1,0:T(8,128)(2,1)S(1)}, bf16[4,16,2560]{2,1,0:T(8,128)(2,1)S(1)}, u32[]{:S(2)}, u32[]{:S(2)}) collective-permute-start(bf16[4,16,2560]{2,1,0:T(8,128)(2,1)S(1)} %bitcast.37), channel_id=1, source_target_pairs={{0,5},{1,4},{2,7},{3,6},{4,1},{5,0},{6,3},{7,2},{8,13},{9,12},{10,... | collective-permute-start | bytes 983048 | tf_op jit(solution)/shard_map/ppermute | solution.py:825
  40.3 17.0 %collective-permute-start.13 = (bf16[4,16,2560]{2,1,0:T(8,128)(2,1)S(1)}, bf16[4,16,2560]{2,1,0:T(8,128)(2,1)S(1)}, u32[]{:S(2)}, u32[]{:S(2)}) collective-permute-start(bf16[4,16,2560]{2,1,0:T(8,128)(2,1)S(1)} %bitcast.38), channel_id=1, source_target_pairs={{0,4},{1,5},{2,6},{3,7},{4,0},{5,1},{6,2},{7,3},{8,12},{9,13},{10,... | collective-permute-start | bytes 983048 | tf_op jit(solution)/shard_map/ppermute | solution.py:825
  40.7 18.5 %collective-permute-start.12 = (bf16[4,16,2560]{2,1,0:T(8,128)(2,1)S(1)}, bf16[4,16,2560]{2,1,0:T(8,128)(2,1)S(1)}, u32[]{:S(2)}, u32[]{:S(2)}) collective-permute-start(bf16[4,16,2560]{2,1,0:T(8,128)(2,1)S(1)} %bitcast.39), channel_id=1, source_target_pairs={{0,1},{1,0},{2,3},{3,2},{4,5},{5,4},{6,7},{7,6},{8,9},{9,8},{10,11... | collective-permute-start | bytes 983048 | tf_op jit(solution)/shard_map/ppermute | solution.py:825
  51.7 8.1 %collective-permute-start.15 = (bf16[4,16,2560]{2,1,0:T(8,128)(2,1)S(1)}, bf16[4,16,2560]{2,1,0:T(8,128)(2,1)S(1)}, u32[]{:S(2)}, u32[]{:S(2)}) collective-permute-start(bf16[4,16,2560]{2,1,0:T(8,128)(2,1)S(1)} %bitcast.40), channel_id=1, source_target_pairs={{0,2},{1,3},{2,0},{3,1},{4,6},{5,7},{6,4},{7,5},{8,10},{9,11},{10,... | collective-permute-start | bytes 983048 | tf_op jit(solution)/shard_map/ppermute | solution.py:825
  59.2 1.6 collective-permute-start.16
  59.2 2.1 collective-permute-start.17
  59.8 2.1 collective-permute-start.18
  131.4 70.4 %reduce-scatter.10.cloned.1.call-start = ((), (), s32[]{:S(2)}) async-start(), calls=%async_computation.7 | async-start | bytes 2621440
  156.8 1.3 copy-start.12
  156.8 73.8 %reduce-scatter.8.cloned.1.call-start = ((), (), s32[]{:S(2)}) async-start(), calls=%async_computation.5 | async-start | bytes 655360 | tf_op jit(solution)/shard_map/reduce_scatter | solution.py:897
  158.1 13.8 %collective-permute-start.19 = (bf16[16,16,2560]{2,1,0:T(8,128)(2,1)S(1)}, bf16[16,16,2560]{2,1,0:T(8,128)(2,1)S(1)}, u32[]{:S(2)}, u32[]{:S(2)}) collective-permute-start(bf16[16,16,2560]{2,1,0:T(8,128)(2,1)S(1)} %copy-done.12), channel_id=1, source_target_pairs={{0,2},{1,3},{2,0},{3,1},{4,6},{5,7},{6,4},{7,5},{8,10},{9,11},{10,... | collective-permute-start | bytes 3932168 | tf_op jit(solution)/shard_map/ppermute | solution.py:825
  173.7 0.7 copy-start.2
  174.4 12.5 %collective-permute-start.20 = (bf16[4,16,2560]{2,1,0:T(8,128)(2,1)S(1)}, bf16[4,16,2560]{2,1,0:T(8,128)(2,1)S(1)}, u32[]{:S(2)}, u32[]{:S(2)}) collective-permute-start(bf16[4,16,2560]{2,1,0:T(8,128)(2,1)S(1)} %get-tuple-element.139), channel_id=1, source_target_pairs={{0,1},{1,0},{2,3},{3,2},{4,5},{5,4},{6,7},{7,6},{8,9},{9,8},{10,11... | collective-permute-start | bytes 983048 | tf_op jit(solution)/shard_map/ppermute | solution.py:825
  175.2 11.9 %copy-start.10 = (f32[3,4,8,128]{3,2,1,0:T(8,128)S(1)}, f32[3,4,8,128]{3,2,1,0:T(8,128)}, u32[]{:S(2)}) copy-start(f32[3,4,8,128]{3,2,1,0:T(8,128)} %get-tuple-element.176) | copy-start | bytes 147460
  186.9 8.8 %collective-permute-start.21 = (bf16[16,16,1664]{2,1,0:T(8,128)(2,1)}, bf16[16,16,1664]{2,1,0:T(8,128)(2,1)S(1)}, u32[]{:S(2)}, u32[]{:S(2)}) collective-permute-start(bf16[16,16,1664]{2,1,0:T(8,128)(2,1)} %get-tuple-element.140), channel_id=1, source_target_pairs={{0,2},{1,3},{2,0},{3,1},{4,6},{5,7},{6,4},{7,5},{8,10},{9,11},{10,... | collective-permute-start | bytes 2555912 | tf_op jit(solution)/shard_map/ppermute | solution.py:825
  187.2 21.6 %collective-permute-start.25 = (bf16[4,16,2560]{2,1,0:T(8,128)(2,1)S(1)}, bf16[4,16,2560]{2,1,0:T(8,128)(2,1)S(1)}, u32[]{:S(2)}, u32[]{:S(2)}) collective-permute-start(bf16[4,16,2560]{2,1,0:T(8,128)(2,1)S(1)} %get-tuple-element.146), channel_id=1, source_target_pairs={{0,4},{1,5},{2,6},{3,7},{4,0},{5,1},{6,2},{7,3},{8,12},{9,13},{10,... | collective-permute-start | bytes 983048 | tf_op jit(solution)/shard_map/ppermute | solution.py:825
  187.8 21.0 %collective-permute-start.26 = (bf16[4,16,2560]{2,1,0:T(8,128)(2,1)S(1)}, bf16[4,16,2560]{2,1,0:T(8,128)(2,1)S(1)}, u32[]{:S(2)}, u32[]{:S(2)}) collective-permute-start(bf16[4,16,2560]{2,1,0:T(8,128)(2,1)S(1)} %get-tuple-element.147), channel_id=1, source_target_pairs={{0,5},{1,4},{2,7},{3,6},{4,1},{5,0},{6,3},{7,2},{8,13},{9,12},{10,... | collective-permute-start | bytes 983048 | tf_op jit(solution)/shard_map/ppermute | solution.py:825
  190.0 1.2 copy-start
  195.7 5.9 %copy-start.6 = (f32[3,16,128]{2,1,0:T(8,128)S(1)}, f32[3,16,128]{2,1,0:T(8,128)}, u32[]{:S(2)}) copy-start(f32[3,16,128]{2,1,0:T(8,128)} %get-tuple-element.175) | copy-start | bytes 73732
  195.7 5.9 %copy-start.7 = (f32[3,16,128]{2,1,0:T(8,128)S(1)}, f32[3,16,128]{2,1,0:T(8,128)}, u32[]{:S(2)}) copy-start(f32[3,16,128]{2,1,0:T(8,128)} %get-tuple-element.174) | copy-start | bytes 73732
  195.7 5.9 %copy-start.8 = (f32[3,16,128]{2,1,0:T(8,128)S(1)}, f32[3,16,128]{2,1,0:T(8,128)}, u32[]{:S(2)}) copy-start(f32[3,16,128]{2,1,0:T(8,128)} %get-tuple-element.173) | copy-start | bytes 73732
  198.0 10.8 %collective-permute-start.22 = (bf16[4,16,1664]{2,1,0:T(8,128)(2,1)}, bf16[4,16,1664]{2,1,0:T(8,128)(2,1)S(1)}, u32[]{:S(2)}, u32[]{:S(2)}) collective-permute-start(bf16[4,16,1664]{2,1,0:T(8,128)(2,1)} %get-tuple-element.143), channel_id=1, source_target_pairs={{0,1},{1,0},{2,3},{3,2},{4,5},{5,4},{6,7},{7,6},{8,9},{9,8},{10,11... | collective-permute-start | bytes 638984 | tf_op jit(solution)/shard_map/ppermute | solution.py:825
  198.8 14.6 %collective-permute-start.23 = (bf16[4,16,1664]{2,1,0:T(8,128)(2,1)S(1)}, bf16[4,16,1664]{2,1,0:T(8,128)(2,1)S(1)}, u32[]{:S(2)}, u32[]{:S(2)}) collective-permute-start(bf16[4,16,1664]{2,1,0:T(8,128)(2,1)S(1)} %get-tuple-element.144), channel_id=1, source_target_pairs={{0,4},{1,5},{2,6},{3,7},{4,0},{5,1},{6,2},{7,3},{8,12},{9,13},{10,... | collective-permute-start | bytes 638984 | tf_op jit(solution)/shard_map/ppermute | solution.py:825
  199.4 14.0 %collective-permute-start.24 = (bf16[4,16,1664]{2,1,0:T(8,128)(2,1)S(1)}, bf16[4,16,1664]{2,1,0:T(8,128)(2,1)S(1)}, u32[]{:S(2)}, u32[]{:S(2)}) collective-permute-start(bf16[4,16,1664]{2,1,0:T(8,128)(2,1)S(1)} %get-tuple-element.145), channel_id=1, source_target_pairs={{0,5},{1,4},{2,7},{3,6},{4,1},{5,0},{6,3},{7,2},{8,13},{9,12},{10,... | collective-permute-start | bytes 638984 | tf_op jit(solution)/shard_map/ppermute | solution.py:825
  201.8 1.0 copy-start.1
  202.8 10.7 %copy-start.3 = (bf16[4,16,2560]{2,1,0:T(8,128)(2,1)S(1)}, bf16[4,16,2560]{2,1,0:T(8,128)(2,1)}, u32[]{:S(2)}) copy-start(bf16[4,16,2560]{2,1,0:T(8,128)(2,1)} %copy-done.2) | copy-start | bytes 983044
  215.9 16.5 %collective-permute-start.27 = (bf16[16,4224]{1,0:T(8,128)(2,1)S(1)}, bf16[16,4224]{1,0:T(8,128)(2,1)S(1)}, u32[]{:S(2)}, u32[]{:S(2)}) collective-permute-start(bf16[16,4224]{1,0:T(8,128)(2,1)S(1)} %get-tuple-element.153), channel_id=1, source_target_pairs={{0,8},{1,9},{2,10},{3,11},{4,12},{5,13},{6,14},{7,15},{8,0},{9,1},... | collective-permute-start | bytes 405512 | tf_op jit(solution)/shard_map/ppermute | solution.py:825
  217.3 15.1 %collective-permute-start.28 = (bf16[16,4224]{1,0:T(8,128)(2,1)S(1)}, bf16[16,4224]{1,0:T(8,128)(2,1)S(1)}, u32[]{:S(2)}, u32[]{:S(2)}) collective-permute-start(bf16[16,4224]{1,0:T(8,128)(2,1)S(1)} %get-tuple-element.154), channel_id=1, source_target_pairs={{0,16},{1,17},{2,18},{3,19},{4,20},{5,21},{6,22},{7,23},{8,24},{9,... | collective-permute-start | bytes 405512 | tf_op jit(solution)/shard_map/ppermute | solution.py:825
  218.4 14.0 %collective-permute-start.29 = (bf16[16,4224]{1,0:T(8,128)(2,1)S(1)}, bf16[16,4224]{1,0:T(8,128)(2,1)S(1)}, u32[]{:S(2)}, u32[]{:S(2)}) collective-permute-start(bf16[16,4224]{1,0:T(8,128)(2,1)S(1)} %get-tuple-element.155), channel_id=1, source_target_pairs={{0,24},{1,25},{2,26},{3,27},{4,28},{5,29},{6,30},{7,31},{8,16},{9,... | collective-permute-start | bytes 405512 | tf_op jit(solution)/shard_map/ppermute | solution.py:825
  220.3 10.1 %copy-start.11 = (f32[3,8,128]{2,1,0:T(8,128)S(1)}, f32[3,8,128]{2,1,0:T(8,128)}, u32[]{:S(2)}) copy-start(f32[3,8,128]{2,1,0:T(8,128)} %get-tuple-element.170) | copy-start | bytes 36868
  220.4 10.1 %copy-start.5 = (s32[12,128]{1,0:T(8,128)S(1)}, s32[12,128]{1,0:T(8,128)}, u32[]{:S(2)}) copy-start(s32[12,128]{1,0:T(8,128)} %refs_4_.7) | copy-start | bytes 18436
  220.4 14.5 %copy-start.9 = (s32[12,256]{1,0:T(8,128)S(1)}, s32[12,256]{1,0:T(8,128)}, u32[]{:S(2)}) copy-start(s32[12,256]{1,0:T(8,128)} %refs_2_.7) | copy-start | bytes 36868
  230.6 0.9 copy-start.4
  234.9 10.4 %all-to-all-start = ((f32[32,1,128]{2,1,0:T(1,128)}), f32[32,1,128]{2,1,0:T(1,128)S(1)}, u32[]{:S(2)}, u32[]{:S(2)}) async-start(f32[32,1,128]{2,1,0:T(1,128)} %bitcast.28), calls=%async_computation.2 | async-start | bytes 32768 | tf_op jit(solution)/shard_map/all_to_all | solution.py:933
Sparse Core Ops, SparseCore 0:
  11.6 70.9 all-gather.2
  131.5 10.5 reduce-scatter.5
  157.0 34.0 reduce-scatter.9
  201.9 20.0 reduce-scatter.7

commit v2 on v1

--- a/solution.py
+++ b/solution.py
@@ -21,7 +21,7 @@
 LANES = 128
 STEP_ROWS = 4
 SMALL_ROWS = 4
-VMEM_LIMIT = 60 * 2**20
+VMEM_LIMIT = 62 * 2**20
 SHARED_LIMIT = 48 * 2**20
 
 COLUMN = (0, 8, 16, 24)
@@ -292,7 +292,7 @@
 def feed_kernel(after_ref, cotangent_ref, dec_ref, padding_ref, gains_ref, gathered_ref,
                 result_ref, branch_b_ref, slots_ref, total_ref, square_ref, token_ref, w_in_ref,
                 w_out_ref, normed_ref, branch_ref, normed_flip, branch_flip, active_ref, grad_ref,
-                in_slots, out_slots, load_sems, sems):
+                in_slots, out_slots, result_tile, branch_tile, load_sems, sems, end_sems):
     part = pl.program_id(0)
     parts = pl.num_programs(0)
     count, length = dec_ref.shape
@@ -375,12 +375,16 @@
         segments = dec_ref[...].astype(F32)
         columns = token_columns(segments)
         total_ref[...] = jnp.zeros_like(total_ref)
+        ends = []
         w_in, w_out = w_in_ref[...].reshape(width, ff), w_out_ref[...].reshape(ff, width)
         for t, rows in enumerate(tiles):
             values = after_ref[rows, :].astype(F32)
-            result_ref[rows, :] = (values + nn(active_ref[rows, :], w_out)).astype(BF16)
+            result_tile[rows, :] = (values + nn(active_ref[rows, :], w_out)).astype(BF16)
             grad, terms = norm_back(values, gains_ref[2:3, :], nt(grad_ref[rows, :], w_in))
-            branch_b_ref[rows, :] = (branch_ref[rows, :].astype(F32) + grad).astype(BF16)
+            branch_tile[rows, :] = (branch_ref[rows, :].astype(F32) + grad).astype(BF16)
+            pairs = [(result_tile.at[rows], result_ref.at[rows])]
+            pairs.append((branch_tile.at[rows], branch_b_ref.at[rows]))
+            ends.extend(start_copies(pairs, end_sems.at[t]))
             own = segments[t * STEP_ROWS : (t + 1) * STEP_ROWS]
             gain_sums(terms, own, total_ref, square_ref.at[t])
         for r in range(count):
@@ -390,7 +394,7 @@
             token_ref[r // STEP_ROWS, r % STEP_ROWS : r % STEP_ROWS + 1, :] = same_sum(
                 products, segments, columns, r
             )
-        for copy in sends(part):
+        for copy in sends(part) + ends:
             copy.wait()
 
 
@@ -402,7 +406,7 @@
 
 def cross_backward_kernel(me_ref, branch_ref, middle_ref, memory_ref, attended_a_ref, input_ref,
                           query_ref, kv_ref, prob_ref, attended_ref, dec_ref, gains_ref,
-                          weight_ref, grad_query_ref, grad_kv_ref, branch_a_ref, low_ref, high_ref,
+                          query_w_ref, out_w_ref, grad_query_ref, grad_kv_ref, branch_a_ref, low_ref, high_ref,
                           total_ref, square_ref, grad_w, grad_attended):
     step = pl.program_id(0)
     mem_length = prob_ref.shape[2]
@@ -415,7 +419,7 @@
         total_ref[...] = jnp.zeros_like(total_ref)
 
     branch = branch_ref[...]
-    grad_attended[...] = nt(branch, weight_ref[:, 4 * width :]).astype(BF16)
+    grad_attended[...] = nt(branch, out_w_ref[...]).astype(BF16)
 
     def places(item):
         r, p = item
@@ -446,7 +450,7 @@
 
     pipelined(row_pairs(STEP_ROWS), enter, bend, leave)
     grad_query = grad_query_ref[...]
-    grad_normed = nt(grad_query, weight_ref[:, width : 2 * width])
+    grad_normed = nt(grad_query, query_w_ref[...])
     grad, terms = norm_back(middle_ref[...].astype(F32), gains_ref[1:2, :], grad_normed)
     branch_a = (branch.astype(F32) + grad).astype(BF16)
     branch_a_ref[...] = branch_a
@@ -461,17 +465,22 @@
         store_slots(me_ref, low_ref, high_ref, partial(read_rows, grad_w))
 
 
-def self_scores_kernel(branch_ref, qkv_ref, prob_ref, dec_ref, buckets_ref, weight_ref,
-                       grad_qkv_ref, table_ref, table_square_ref, grad_attended, bands):
+def self_backward_kernel(me_ref, branch_ref, tokens_ref, input_ref, qkv_ref, prob_ref, dec_ref,
+                         buckets_ref, gains_ref, out_w_ref, weight_ref, total_b_ref, total_c_ref,
+                         grad_qkv_ref, grad_tokens_ref, low_ref, high_ref, square_ref,
+                         table_square_ref, grad_w, total_ref, small_ref, table_ref, grad_attended,
+                         bands):
     step = pl.program_id(0)
     length = prob_ref.shape[2]
     width = branch_ref.shape[1]
-    grad_attended[...] = nt(branch_ref[...], weight_ref[:, :width]).astype(BF16)
+    grad_attended[...] = nt(branch_ref[...], out_w_ref[...]).astype(BF16)
 
     @pl.when(step == 0)
     def _():
         table_ref[...] = jnp.zeros_like(table_ref)
         bands[...] = jnp.zeros_like(bands)
+        grad_w[...] = jnp.zeros_like(grad_w)
+        total_ref[...] = jnp.zeros_like(total_ref)
 
     row_i = lax.broadcasted_iota(jnp.int32, (length, length), 0)
     col_i = lax.broadcasted_iota(jnp.int32, (length, length), 1)
@@ -534,22 +543,10 @@
     squares = jnp.sum(jnp.sum(per_bucket * per_bucket, axis=1), axis=-1, keepdims=True)
     table_square_ref[0] = jnp.broadcast_to(squares, (STEP_ROWS, 8, LANES))
 
-
-def self_weights_kernel(me_ref, branch_ref, tokens_ref, input_ref, grad_qkv_ref, dec_ref,
-                        gains_ref, weight_ref, table_ref, total_b_ref, total_c_ref,
-                        grad_tokens_ref, low_ref, high_ref, square_ref, grad_w, total_ref,
-                        small_ref):
-    step = pl.program_id(0)
-    width = tokens_ref.shape[1]
     grad_qkv = grad_qkv_ref[...]
-    grad_normed = nt(grad_qkv, weight_ref[:, : 3 * width])
+    grad_normed = nt(grad_qkv, weight_ref[...])
     grad, terms = norm_back(tokens_ref[...].astype(F32), gains_ref[0:1, :], grad_normed)
     grad_tokens_ref[...] = (branch_ref[...].astype(F32) + grad).astype(BF16)
-
-    @pl.when(step == 0)
-    def _():
-        grad_w[...] = jnp.zeros_like(grad_w)
-        total_ref[...] = jnp.zeros_like(total_ref)
 
     gain_sums(terms, step_rows(dec_ref, step, STEP_ROWS), total_ref, square_ref.at[0])
     flipped = input_ref[...].T
@@ -578,54 +575,59 @@
         store_slots(me_ref, low_ref, high_ref, read)
 
 
-def pair_sum_kernel(low_ref, sent_ref, *refs):
-    outs, (low, sent, total, load_sems, store_sems) = refs[:4], refs[4:]
+def pair_sum_kernel(*refs):
+    groups, outs, buffers, total = (refs[:2], refs[2:4]), refs[4:8], refs[8:12], refs[12]
+    load_sems, store_sems = refs[13:]
     places = [pl.ds(4 * t, 4) for t in range(4)]
-    lows = start_copies([(low_ref.at[p], low.at[p]) for p in places], load_sems.at[0])
-    sents = start_copies([(sent_ref.at[p], sent.at[p]) for p in places], load_sems.at[1])
+    loads = []
+    for i, ref in enumerate((*groups[0], *groups[1])):
+        pairs = [(ref.at[p], buffers[i].at[p]) for p in places]
+        loads.append(start_copies(pairs, load_sems.at[i]))
     stores = []
     for t, p in enumerate(places):
-        lows[t].wait()
-        sents[t].wait()
-        total[p] = (low[p].astype(F32) + sent[p].astype(F32)).astype(BF16)
+        start = 0
+        for low, sent in ((0, 1), (2, 3)):
+            loads[low][t].wait()
+            loads[sent][t].wait()
+            own = buffers[low][p].astype(F32) + buffers[sent][p].astype(F32)
+            total[p, :, start : start + own.shape[2]] = own.astype(BF16)
+            start += own.shape[2]
         stores.append(pltpu.make_async_copy(total.at[p], outs[t], store_sems.at[t]))
         stores[t].start()
     for store in stores:
         store.wait()
 
 
-def pair_sum(low, sent, after):
-    piece = shape_of((4,) + low.shape[1:], BF16)
+def pair_sum(groups):
+    arrays = [array for group in groups for array in group]
+    lanes = sum(low.shape[2] for low, _ in groups)
+    shape = arrays[0].shape[:2] + (lanes,)
     return pl.pallas_call(
-        ignoring(pair_sum_kernel, 2, len(after)),
-        out_shape=(piece,) * 4,
-        in_specs=[pl.BlockSpec(memory_space=pl.ANY)] * (2 + len(after)),
+        pair_sum_kernel,
+        out_shape=(shape_of((4,) + shape[1:], BF16),) * 4,
+        in_specs=[pl.BlockSpec(memory_space=pl.ANY)] * 4,
         out_specs=[pl.BlockSpec(memory_space=pl.ANY)] * 4,
-        scratch_shapes=[pltpu.VMEM(low.shape, BF16)] * 3
-        + [pltpu.SemaphoreType.DMA((2, 4)), pltpu.SemaphoreType.DMA((4,))],
+        scratch_shapes=[pltpu.VMEM(array.shape, BF16) for array in arrays]
+        + [pltpu.VMEM(shape, BF16)]
+        + [pltpu.SemaphoreType.DMA((4, 4)), pltpu.SemaphoreType.DMA((4,))],
         compiler_params=pltpu.CompilerParams(vmem_limit_bytes=SHARED_LIMIT),
-    )(in_hbm(low), sent, *after)
-
-
-def plane_sum_kernel(*refs):
-    own_ref, outs = refs[8], refs[9:]
-    start = 0
-    for group in (refs[:4], refs[4:8]):
-        cols = slice(start, start + group[0].shape[2])
-        start = cols.stop
-        for s in range(4):
-            total = sum(ref[s].astype(F32) for ref in group)
-            if s == 0:
-                own_ref[:, cols] = total
-            else:
-                outs[s - 1][:, cols] = total.astype(BF16)
-
-
-def plane_sum(groups, after):
-    line = (16, sum(group[0].shape[2] for group in groups))
+    )(*[in_hbm(a) if i % 2 == 0 else a for i, a in enumerate(arrays)])
+
+
+def plane_sum_kernel(a_ref, b_ref, c_ref, d_ref, own_ref, *outs):
+    for s in range(4):
+        total = a_ref[s].astype(F32) + b_ref[s].astype(F32)
+        total = total + c_ref[s].astype(F32) + d_ref[s].astype(F32)
+        if s == 0:
+            own_ref[...] = total
+        else:
+            outs[s - 1][...] = total.astype(BF16)
+
+
+def plane_sum(pieces, after):
+    line = pieces[0].shape[1:]
     return small_call(
-        plane_sum_kernel, [*groups[0], *groups[1]], after,
-        (shape_of(line, F32),) + (shape_of(line, BF16),) * 3,
+        plane_sum_kernel, pieces, after, (shape_of(line, F32),) + (shape_of(line, BF16),) * 3
     )
 
 
@@ -727,7 +729,7 @@
     for first in range(0, width, 256):
         rows = slice(first, first + 256)
         grad_memory_ref[:, rows] = nt(
-            grad_kv_ref[...], weight_ref[rows, 2 * width : 4 * width]
+            grad_kv_ref[...], weight_ref[rows, :]
         ).astype(BF16)
     count = memory_ref.shape[0] // mem_length
     segments = step_rows(mem_ref, pl.program_id(0), count)
@@ -758,6 +760,11 @@
     return pl.BlockSpec(shape, lambda i, *_: (i,) + (0,) * (len(shape) - 1))
 
 
+class Cut:
+    def __init__(self, array, shape, *index):
+        self.array, self.spec = array, pl.BlockSpec(shape, lambda i, *_: index)
+
+
 def whole_spec(array):
     return pl.BlockSpec(array.shape, lambda i, *_: (0,) * len(array.shape))
 
@@ -776,6 +783,10 @@
     blocked, whole = list(blocked), list(whole)
     for kind in order[0]:
         array = (blocked if kind == "i" else whole).pop(0)
+        if isinstance(array, Cut):
+            ins.append(array.array)
+            in_specs.append(array.spec)
+            continue
         ins.append(array)
         in_specs.append(rows_spec(array, steps) if kind == "i" else whole_spec(array))
     ins = [in_hbm(array) for array in ins]
@@ -1007,17 +1018,20 @@
             *[pltpu.VMEM((dec, ff), BF16)] * 2,
             pltpu.VMEM((32, 16, width), BF16),
             pltpu.VMEM((8, 64, width), BF16),
+            *[pltpu.VMEM((dec, width), BF16)] * 2,
             dma((4, 2)),
             dma((9,)),
+            dma((steps, 2)),
         ],
-        26 * flops, ("wwwww", "wwawww"),
+        26 * flops, ("wwwww", "aaawww"),
     )
     feed_sum = way.feed_core(feed_slots)
     slot = shape_of((16, 16, 5 * width), BF16)
     grad_query_b, grad_kv_b, branch_a, cross_low, cross_high, gain_b, square_b = call(
         cross_backward_kernel, steps, me,
         (branch_b, middle, memory2, attended_a, input_b, query_b, kv_b, prob_b, attended_b),
-        (dec_segments, gains, cross_w), (),
+        (dec_segments, gains, Cut(cross_w, (width, width), 0, 1),
+         Cut(cross_w, (width, width), 0, 4)), (),
         (
             kept((dec, width), BF16),
             kept((mem, 2 * width), BF16),
@@ -1026,37 +1040,34 @@
         ),
         (kept(slot.shape, BF16), slot, total),
         [pltpu.VMEM((width, 5 * width), F32), pltpu.VMEM((step_dec, width), BF16)],
-        20 * flops, ("iiiiiiiiiwww", "iiiwwwi"),
+        20 * flops, ("iiiiiiiiiwwww", "iiiwwwi"),
     )
     feed_sum = way.feed_plane(hold(feed_sum, grad_query_b))
     near = isinstance(way, Near)
     if near:
         sent = shift(cross_high, 2)
-    grad_qkv_a, table, table_square = call(
-        self_scores_kernel, steps, None, (branch_a, qkv_a, prob_a),
-        (dec_segments, buckets, cross_w), (),
-        (kept((dec, 3 * width), BF16), shape_of((steps, STEP_ROWS, 8, LANES), F32)),
-        (kept((H, LANES), F32),),
-        [pltpu.VMEM((step_dec, width), BF16), pltpu.VMEM((STEP_ROWS, H, 8, length), F32)],
-        10 * flops, ("iiiwww", "iwi"),
-    )
-    waits = ()
-    if near:
-        cross_parts = pair_sum(cross_low, sent, (grad_qkv_a,))
-        crossed = shift_plane(cross_parts[1:])
-        waits = (cross_parts[0],)
     slot = shape_of((16, 16, 3 * width + LANES), BF16)
-    grad_tokens, self_low, self_high, square_a = call(
-        self_weights_kernel, steps, me, (branch_a, tokens2, input_a, grad_qkv_a),
-        (dec_segments, gains, self_w, table, gain_b, gain_c), (),
-        (shape_of((dec, width), BF16), square),
+    grad_qkv_a, grad_tokens, self_low, self_high, square_a, table_square = call(
+        self_backward_kernel, steps, me, (branch_a, tokens2, input_a, qkv_a, prob_a),
+        (dec_segments, buckets, gains, Cut(cross_w, (width, width), 0, 0),
+         Cut(self_w, (width, 3 * width), 0, 0), gain_b, gain_c),
+        (),
+        (
+            kept((dec, 3 * width), BF16),
+            shape_of((dec, width), BF16),
+            square,
+            shape_of((steps, STEP_ROWS, 8, LANES), F32),
+        ),
         (kept(slot.shape, BF16), slot),
         [
             pltpu.VMEM((width, 3 * width), F32),
             pltpu.VMEM((1, width), F32),
             pltpu.VMEM((width, LANES), F32),
+            pltpu.VMEM((H, LANES), F32),
+            pltpu.VMEM((step_dec, width), BF16),
+            pltpu.VMEM((STEP_ROWS, H, 8, length), F32),
         ],
-        7 * flops, ("iiiiwwwwww", "iwwi"), waits,
+        17 * flops, ("iiiiiwwwwwww", "iiwwii"),
     )
 
     def grams(pairs, *after):
@@ -1075,35 +1086,34 @@
     def fill_memory(*after):
         return call(
             memory_backward_kernel, small_steps, None, (memory2, grad_kv_b),
-            (mem_segments, cross_w), (),
+            (mem_segments, Cut(cross_w, (width, 2 * width), 0, 1)), (),
             (shape_of((mem, width), BF16), shape_of((small_steps, 8, mem_length), F32)), (), [],
             10 * flops, ("iiww", "ii"), after, SHARED_LIMIT,
         )
 
     if near:
-        sent = shift(hold(self_high, crossed[0]), 2)
-        token_b = fill_cross(self_low)
-        self_parts = pair_sum(self_low, sent, (token_b,))
-        self_sent = shift_plane(self_parts[1:])
+        self_sent = shift(self_high, 2)
+        parts = pair_sum(((self_low, self_sent), (cross_low, sent)))
+        crossed = shift_plane(parts[1:])
+        token_b = fill_cross(parts[0])
         feed_sum = hold(feed_sum, token_b)
-        token_a = fill_self(self_parts[0], feed_sum)
+        grad_memory, token_m = fill_memory(feed_sum)
         feed_sum = way.feed_column(feed_sum)
-        groups = [[self_parts[0], *self_sent], [cross_parts[0], *crossed]]
-        own, *rest = plane_sum(groups, (token_a,))
+        own, *rest = plane_sum([parts[0], *crossed], (token_m,))
         line_sent = shift_column(rest)
-        grad_memory, token_m = fill_memory(own)
-        feed_sum = hold(feed_sum, token_m).reshape(128, width)
+        token_a = fill_self(own)
+        feed_sum = hold(feed_sum, token_a).reshape(128, width)
         grad_hidden, grad_back, square = small_call(
-            feed_end_kernel, (feed_sum,), (token_m,),
+            feed_end_kernel, (feed_sum,), (token_a,),
             [shape_of((16, ff), F32), shape_of((64, width), F32), shape_of((8, LANES), F32)],
         )
         line = shape_of((slot.shape[1], width), F32)
         *parts, square = small_call(
-            column_end_kernel, (own, *line_sent, square), (token_m,),
+            column_end_kernel, (own, *line_sent, square), (token_a,),
             [line] * 3 + [shape_of((16, LANES), F32)] + [line] * 5 + [shape_of((32, LANES), F32)],
         )
         self_grads, small, cross_grads = parts[:3], parts[3], parts[4:]
-        token_m = hold(token_m, square)
+        token_a = hold(token_a, square)
     else:
         token_b, token_a = fill_cross(), fill_self()
         grad_memory, token_m = fill_memory()

time: 256 us -> 254 us (level)
  waiting for transfers between devices: 34 us -> 46.7 us
  Pallas kernels: 163 us -> 154 us
  local copies, waits for them, and re-layouts: 7.18 us -> 4.09 us
    ppermute x30 -> x27, waiting for transfers between devices: 27.7 us -> 38.9 us  [shift(): return lax.ppermute(array, FINE, [(i, i ^ mask) for i in range(32)])]
    pallas_call x9 -> x8, Pallas kernels: 151 us -> 143 us  [call(): pl.pallas_call(kernel, out_shape=outs, grid_spec=pltpu.PrefetchScalarGrid...]
    ppermute x30 -> x27, starting transfers between devices: 29.3 us -> 26 us  [shift(): return lax.ppermute(array, FINE, [(i, i ^ mask) for i in range(32)])]
    unnamed x27 -> x17, local copies, waits for them, and re-layouts: 5.71 us -> 2.63 us
  transfers between devices with their start and end apart: 35 -> 32, of which waited for: 13 -> 17; matrix products, arithmetic and copies ran while one was open for 1% -> 1% of each run, Pallas kernels for 43% -> 40%
where the time goes in v2:
time: 254 us; the launch traced here: 253 us
  Pallas kernels  154 us (61%)
  waiting for transfers between devices  46.7 us (18%)
  starting transfers between devices  30.4 us (12%)
  between operations  16 us (6%)
  local copies, waits for them, and re-layouts  4.09 us (2%)
    pallas_call x8, Pallas kernels, call(): pl.pallas_call(kernel, out_shape=outs, grid_spec=pltpu.PrefetchScalarGrid...  143 us
    ppermute x27, waiting for transfers between devices, shift(): return lax.ppermute(array, FINE, [(i, i ^ mask) for i in range(32)])  38.9 us
    ppermute x27, starting transfers between devices, shift(): return lax.ppermute(array, FINE, [(i, i ^ mask) for i in range(32)])  26 us
    all_to_all x1, waiting for transfers between devices, on_device(): sent = lax.all_to_all(square, FINE, 0, 0, tiled=True)  6.01 us
    pallas_call x4, Pallas kernels, small_call(): pl.pallas_call(ignoring(staged(kernel, len(ins), len(outs)), len(ins), le...  5.58 us
  transfers between devices with their start and end apart: 32, of which 17 were waited for; matrix products, arithmetic and copies ran while one was open for 1% of the time, Pallas kernels for 40%

profile of v2, /device:TPU:0, one launch (start us, length us, event | category | flops | bytes accessed | tf_op | source)
XLA Modules:
  0.0 253.1 jit_solution(10825194727371476251)
XLA Ops:
  7.2 0.8 fusion.2
  8.0 2.0 shard_map.348
  10.1 5.1 %collective-permute-start.2 = (bf16[16,1664]{1,0:T(8,128)(2,1)S(1)}, bf16[16,1664]{1,0:T(8,128)(2,1)S(1)}, u32[]{:S(2)}, u32[]{:S(2)}) collective-permute-start(bf16[16,1664]{1,0:T(8,128)(2,1)S(1)} %get-tuple-element.92.refs_0_), channel_id=1, source_target_pairs={{0,24},{1,25},{2,26},{3,27},{4,28},{5,29},{6,30},{7,31},{8,16},{9,... | collective-permute-start | bytes 159752 | tf_op jit(solution)/shard_map/ppermute | solution.py:836
  15.2 0.6 collective-permute-start
  15.9 1.7 collective-permute-done.2.refs_3_
  17.5 2.7 %collective-permute-done.1.refs_2_ = bf16[16,1664]{1,0:T(8,128)(2,1)S(1)} collective-permute-done((bf16[16,1664]{1,0:T(8,128)(2,1)S(1)}, bf16[16,1664]{1,0:T(8,128)(2,1)S(1)}, u32[]{:S(2)}, u32[]{:S(2)}) %collective-permute-start.1) | collective-permute-done | bytes 53280 | tf_op jit(solution)/shard_map/ppermute | solution.py:836
  20.6 0.9 collective-permute-start.6
  21.5 2.4 collective-permute-start.5
  24.4 0.5 collective-permute-start.3
  25.3 2.1 collective-permute-start.7
  27.4 9.0 %collective-permute-done.7.refs_1_ = bf16[2,16,2560]{2,1,0:T(8,128)(2,1)S(1)} collective-permute-done((bf16[2,16,2560]{2,1,0:T(8,128)(2,1)S(1)}, bf16[2,16,2560]{2,1,0:T(8,128)(2,1)S(1)}, u32[]{:S(2)}, u32[]{:S(2)}) %collective-permute-start.7) | collective-permute-done | bytes 163872 | tf_op jit(solution)/shard_map/ppermute | solution.py:836
  37.8 2.5 collective-permute-start.14
  40.7 0.6 collective-permute-start.12
  41.4 10.3 %shard_map.351 = (bf16[1536,512]{1,0:T(8,128)(2,1)}, bf16[1536,1536]{1,0:T(8,128)(2,1)}, bf16[12,4,128,256]{3,2,1,0:T(8,128)(2,1)}, bf16[1536,512]{1,0:T(8,128)(...) custom-call(s32[1]{0:T(128)} %bitcast.refs_0_, bf16[1536,512]{1,0:T(8,128)(2,1)} %bitcast.56, ...), custom_call_target="tpu_custom_call" | custom-call | flops 4831838208 | bytes 16019968 | tf_op jit(solution)/shard_map/pallas_call | solution.py:807
  51.8 1.3 collective-permute-done.14.refs_10_
  53.1 4.3 %collective-permute-done.13.refs_9_ = bf16[4,16,2560]{2,1,0:T(8,128)(2,1)S(1)} collective-permute-done((bf16[4,16,2560]{2,1,0:T(8,128)(2,1)S(1)}, bf16[4,16,2560]{2,1,0:T(8,128)(2,1)S(1)}, u32[]{:S(2)}, u32[]{:S(2)}) %collective-permute-start.13) | collective-permute-done | bytes 327712 | tf_op jit(solution)/shard_map/ppermute | solution.py:836
  57.4 1.9 collective-permute-done.12.refs_8_
  59.8 1.1 collective-permute-done.16.refs_12_
  61.8 20.6 %shard_map.353 = (bf16[1536,512]{1,0:T(8,128)(2,1)}, bf16[1536,512]{1,0:T(8,128)(2,1)}, bf16[1536,512]{1,0:T(8,128)(2,1)}, bf16[3072,1024]{1,0:T(8,128)(2,1)}, b...) custom-call(s32[1]{0:T(128)} %bitcast.refs_0_, ...), custom_call_target="tpu_custom_call" | custom-call | flops 8053063680 | bytes 32016384 | tf_op jit(solution)/shard_map/pallas_call | solution.py:807
  82.6 47.5 %shard_map.354 = (bf16[1536,512]{1,0:T(8,128)(2,1)}, bf16[1536,512]{1,0:T(8,128)(2,1)}, bf16[32,128,512]{2,1,0:T(8,128)(2,1)}, f32[1,512]{1,0:T(1,128)}, f32[3,16,128]{2,1,0:T(8,128)}, /*index=5*/f32[3,8,128]{2,1,0:T(8,128)}) custom-call(bf16[1536,512]{1,0:T(8,128)(2,1)} %get-tuple-element.106.refs_0_, bf16[1536,512]{1,0:T(8,128)(2,1)} %bitcast.55, ...), custom_call_target="tpu_custom_call" | custom-call | flops 20937965568 | bytes 14747648 | tf_op jit(solution)/shard_map/pallas_call | solution.py:807
  130.1 24.4 %shard_map.355 = (bf16[1536,512]{1,0:T(8,128)(2,1)}, bf16[3072,1024]{1,0:T(8,128)(2,1)}, bf16[1536,512]{1,0:T(8,128)(2,1)}, bf16[16,16,2560]{2,1,0:T(8,128)(2,1)...) custom-call(s32[1]{0:T(128)} %bitcast.refs_0_, ...), custom_call_target="tpu_custom_call" | custom-call | flops 16106127360 | bytes 42516480 | tf_op jit(solution)/shard_map/pallas_call | solution.py:807
  154.9 21.0 %shard_map.356 = (bf16[1536,1536]{1,0:T(8,128)(2,1)}, bf16[1536,512]{1,0:T(8,128)(2,1)}, bf16[16,16,1664]{2,1,0:T(8,128)(2,1)}, bf16[16,16,1664]{2,1,0:T(8,128)(...) custom-call(s32[1]{0:T(128)} %bitcast.refs_0_, bf16[1536,512]{1,0:T(8,128)(2,1)} %get-tuple-element.117.refs_1_.refs_3_, ...), custom_call_target="tpu_custom_call" | custom-call | flops 13690208256 | bytes 25004544 | tf_op jit(solution)/shard_map/pallas_call | solution.py:807
  176.2 0.8 fusion
  177.0 1.5 collective-permute-done.19.refs_1_
  178.5 3.6 %shard_map.357 = (bf16[4,16,4224]{2,1,0:T(8,128)(2,1)S(1)}, bf16[4,16,4224]{2,1,0:T(8,128)(2,1)}, bf16[4,16,4224]{2,1,0:T(8,128)(2,1)}, bf16[4,16,4224]{2,1,0:T(8,128)(2,1)S(1)}) custom-call(bf16[16,16,1664]{2,1,0:T(8,128)(2,1)} %get-tuple-element.129.refs_0_, bf16[16,16,1664]{2,1,0:T(8,128)(2,1)S(1)} %collective-permute-done.19.refs_1_, ...), custom_call_target="tpu_custom_call" | custom-call | tf_op jit(solution)/shard_map/pallas_call | solution.py:605
  182.1 4.6 %shard_map.358 = f32[3,8,128]{2,1,0:T(8,128)S(1)} custom-call(bf16[1536,512]{1,0:T(8,128)(2,1)} %get-tuple-element.111.refs_5_.refs_0_, bf16[1536,512]{1,0:T(8,128)(2,1)} %get-tuple-element.127.refs_1_, bf16[1536,512]{1,0:T(8,128)(2,1)} %get-tuple-element.115.refs_9_.refs_2_, bf16[1536,512]{1,0:T(8,128)(2,1)} %get-tuple-element.109.refs_1_.refs_3_, ...), custom_call_target="tpu_custom_call" | custom-call | flops 1610612736 | bytes 6850560 | tf_op jit(solution)/shard_map/pallas_call | solution.py:807
  186.7 1.5 reduce-scatter.10.cloned.1.call-done
  188.4 1.4 collective-permute-start.21
  189.8 0.6 collective-permute-start.22
  190.4 1.5 collective-permute-start.23
  191.9 1.0 copy-done
  192.9 8.9 %shard_map.359 = (bf16[3072,512]{1,0:T(8,128)(2,1)}, f32[3,8,256]{2,1,0:T(8,128)S(1)}) custom-call(bf16[3072,512]{1,0:T(8,128)(2,1)} %bitcast.54, bf16[3072,1024]{1,0:T(8,128)(2,1)} %get-tuple-element.125.refs_1_, s32[12,256]{1,0:T(8,128)} %refs_2_.7, bf16[512,2560]{1,0:T(8,128)(2,1)} %bitcast.65, bf16[4,128,512]{2,1,0:T(8,128)(2,1)S(1)} %bitcast.36), custom_call_target="tpu_custom_call" | custom-call | flops 8053063680 | bytes 15765504 | tf_op jit(solution)/shard_map/pallas_call | solution.py:807
  201.8 1.9 collective-permute-done.21.refs_1_
  203.8 11.6 %collective-permute-done.22.refs_2_ = bf16[4,16,4224]{2,1,0:T(8,128)(2,1)S(1)} collective-permute-done((bf16[4,16,4224]{2,1,0:T(8,128)(2,1)}, bf16[4,16,4224]{2,1,0:T(8,128)(2,1)S(1)}, u32[]{:S(2)}, u32[]{:S(2)}) %collective-permute-start.22) | collective-permute-done | bytes 540704 | tf_op jit(solution)/shard_map/ppermute | solution.py:836
  215.4 1.1 shard_map.360
  216.5 1.5 collective-permute-start.24
  218.0 2.4 collective-permute-start.25
  221.1 6.4 %shard_map.361.refs_1_.refs_5_ = f32[3,8,128]{2,1,0:T(8,128)S(1)} custom-call(bf16[1536,512]{1,0:T(8,128)(2,1)} %get-tuple-element.118.refs_3_.refs_0_, bf16[1536,1536]{1,0:T(8,128)(2,1)} %get-tuple-element.144.refs_1_, bf16[1536,512]{1,0:T(8,128)(2,1)} %get-tuple-element.99.refs_2_.refs_4_, bf16[1536,512]{1,0:T(8,128)(2,1)} %get-tuple-element.117.refs_1_.refs_3_, ...), custom_call_target="tpu_custom_call" | custom-call | flops 1610612736 | bytes 9725952 | tf_op jit(solution)/shard_map/pallas_call | solution.py:807
  227.5 0.9 copy-done.1
  228.3 0.9 shard_map.362
  229.2 0.8 collective-permute-done.25.refs_2_
  230.1 1.6 shard_map.363
  231.8 0.7 slice_reduce_fusion.2
  232.6 4.2 %all-to-all-start = ((f32[32,1,128]{2,1,0:T(1,128)}), f32[32,1,128]{2,1,0:T(1,128)S(1)}, u32[]{:S(2)}, u32[]{:S(2)}) async-start(f32[32,1,128]{2,1,0:T(1,128)} %bitcast.28), calls=%async_computation.2 | async-start | bytes 32768 | tf_op jit(solution)/shard_map/all_to_all | solution.py:944
  236.8 0.5 slice_bitcast_fusion
  237.3 0.7 copy.53
  238.0 6.0 %all-to-all-done = f32[32,1,128]{2,1,0:T(1,128)S(1)} async-done(((f32[32,1,128]{2,1,0:T(1,128)}), f32[32,1,128]{2,1,0:T(1,128)S(1)}, u32[]{:S(2)}, u32[]{:S(2)}) %all-to-all-start) | async-done | bytes 16416 | tf_op jit(solution)/shard_map/all_to_all | solution.py:944
  244.0 0.6 slice_reduce_fusion.1
  (70 shorter events, 6.6 us)
Async XLA Ops:
  7.2 75.4 %all-gather.3.cloned.1.call-start = ((), (), s32[]{:S(2)}) async-start(), calls=%async_computation.6 | async-start | bytes 4325376 | tf_op jit(solution)/shard_map/all_gather | solution.py:885
  10.1 144.5 %reduce-scatter.6.cloned.1.call-start = ((), (), s32[]{:S(2)}) async-start(), calls=%async_computation.4 | async-start | bytes 6291456 | tf_op jit(solution)/shard_map/reduce_scatter | solution.py:902
  10.1 7.4 %collective-permute-start.2 = (bf16[16,1664]{1,0:T(8,128)(2,1)S(1)}, bf16[16,1664]{1,0:T(8,128)(2,1)S(1)}, u32[]{:S(2)}, u32[]{:S(2)}) collective-permute-start(bf16[16,1664]{1,0:T(8,128)(2,1)S(1)} %get-tuple-element.92.refs_0_), channel_id=1, source_target_pairs={{0,24},{1,25},{2,26},{3,27},{4,28},{5,29},{6,30},{7,31},{8,16},{9,... | collective-permute-start | bytes 159752 | tf_op jit(solution)/shard_map/ppermute | solution.py:836
  15.2 5.0 %collective-permute-start.1 = (bf16[16,1664]{1,0:T(8,128)(2,1)S(1)}, bf16[16,1664]{1,0:T(8,128)(2,1)S(1)}, u32[]{:S(2)}, u32[]{:S(2)}) collective-permute-start(bf16[16,1664]{1,0:T(8,128)(2,1)S(1)} %get-tuple-element.92.refs_0_), channel_id=1, source_target_pairs={{0,16},{1,17},{2,18},{3,19},{4,20},{5,21},{6,22},{7,23},{8,24},{9,... | collective-permute-start | bytes 159752 | tf_op jit(solution)/shard_map/ppermute | solution.py:836
  15.2 5.0 %collective-permute-start = (bf16[16,1664]{1,0:T(8,128)(2,1)S(1)}, bf16[16,1664]{1,0:T(8,128)(2,1)S(1)}, u32[]{:S(2)}, u32[]{:S(2)}) collective-permute-start(bf16[16,1664]{1,0:T(8,128)(2,1)S(1)} %get-tuple-element.92.refs_0_), channel_id=1, source_target_pairs={{0,8},{1,9},{2,10},{3,11},{4,12},{5,13},{6,14},{7,15},{8,0},{9,1},... | collective-permute-start | bytes 159752 | tf_op jit(solution)/shard_map/ppermute | solution.py:836
  20.6 4.5 %collective-permute-start.6 = (bf16[16,2560]{1,0:T(8,128)(2,1)S(1)}, bf16[16,2560]{1,0:T(8,128)(2,1)S(1)}, u32[]{:S(2)}, u32[]{:S(2)}) collective-permute-start(bf16[16,2560]{1,0:T(8,128)(2,1)S(1)} %get-tuple-element.94.refs_0_), channel_id=1, source_target_pairs={{0,8},{1,9},{2,10},{3,11},{4,12},{5,13},{6,14},{7,15},{8,0},{9,1},... | collective-permute-start | bytes 245768 | tf_op jit(solution)/shard_map/ppermute | solution.py:836
  21.5 14.9 %collective-permute-start.5 = (bf16[4,16,1664]{2,1,0:T(8,128)(2,1)S(1)}, bf16[4,16,1664]{2,1,0:T(8,128)(2,1)S(1)}, u32[]{:S(2)}, u32[]{:S(2)}) collective-permute-start(bf16[4,16,1664]{2,1,0:T(8,128)(2,1)S(1)} %shard_map.349.refs_5_), channel_id=1, source_target_pairs={{0,5},{1,4},{2,7},{3,6},{4,1},{5,0},{6,3},{7,2},{8,13},{9,12},{10,... | collective-permute-start | bytes 638984 | tf_op jit(solution)/shard_map/ppermute | solution.py:836
  23.9 12.9 %collective-permute-start.4 = (bf16[4,16,1664]{2,1,0:T(8,128)(2,1)S(1)}, bf16[4,16,1664]{2,1,0:T(8,128)(2,1)S(1)}, u32[]{:S(2)}, u32[]{:S(2)}) collective-permute-start(bf16[4,16,1664]{2,1,0:T(8,128)(2,1)S(1)} %shard_map.349.refs_5_), channel_id=1, source_target_pairs={{0,4},{1,5},{2,6},{3,7},{4,0},{5,1},{6,2},{7,3},{8,12},{9,13},{10,... | collective-permute-start | bytes 638984 | tf_op jit(solution)/shard_map/ppermute | solution.py:836
  24.4 12.5 %collective-permute-start.3 = (bf16[4,16,1664]{2,1,0:T(8,128)(2,1)S(1)}, bf16[4,16,1664]{2,1,0:T(8,128)(2,1)S(1)}, u32[]{:S(2)}, u32[]{:S(2)}) collective-permute-start(bf16[4,16,1664]{2,1,0:T(8,128)(2,1)S(1)} %shard_map.349.refs_5_), channel_id=1, source_target_pairs={{0,1},{1,0},{2,3},{3,2},{4,5},{5,4},{6,7},{7,6},{8,9},{9,8},{10,11... | collective-permute-start | bytes 638984 | tf_op jit(solution)/shard_map/ppermute | solution.py:836
  25.3 11.1 %collective-permute-start.7 = (bf16[2,16,2560]{2,1,0:T(8,128)(2,1)S(1)}, bf16[2,16,2560]{2,1,0:T(8,128)(2,1)S(1)}, u32[]{:S(2)}, u32[]{:S(2)}) collective-permute-start(bf16[2,16,2560]{2,1,0:T(8,128)(2,1)S(1)} %shard_map.350.refs_0_), channel_id=1, source_target_pairs={{0,16},{1,17},{2,18},{3,19},{4,20},{5,21},{6,22},{7,23},{8,24},{9,... | collective-permute-start | bytes 491528 | tf_op jit(solution)/shard_map/ppermute | solution.py:836
  36.3 4.0 %collective-permute-start.8 = (bf16[4,16,1664]{2,1,0:T(8,128)(2,1)S(1)}, bf16[4,16,1664]{2,1,0:T(8,128)(2,1)S(1)}, u32[]{:S(2)}, u32[]{:S(2)}) collective-permute-start(bf16[4,16,1664]{2,1,0:T(8,128)(2,1)S(1)} %shard_map.349.refs_5_), channel_id=1, source_target_pairs={{0,2},{1,3},{2,0},{3,1},{4,6},{5,7},{6,4},{7,5},{8,10},{9,11},{10,... | collective-permute-start | bytes 638984 | tf_op jit(solution)/shard_map/ppermute | solution.py:836
  36.4 4.4 %collective-permute-start.11 = (bf16[4,16,1664]{2,1,0:T(8,128)(2,1)S(1)}, bf16[4,16,1664]{2,1,0:T(8,128)(2,1)S(1)}, u32[]{:S(2)}, u32[]{:S(2)}) collective-permute-start(bf16[4,16,1664]{2,1,0:T(8,128)(2,1)S(1)} %collective-permute-done.5.refs_8_), channel_id=1, source_target_pairs={{0,2},{1,3},{2,0},{3,1},{4,6},{5,7},{6,4},{7,5},{8,10},{9,11},{10,... | collective-permute-start | bytes 638984 | tf_op jit(solution)/shard_map/ppermute | solution.py:836
  36.9 4.5 %collective-permute-start.10 = (bf16[4,16,1664]{2,1,0:T(8,128)(2,1)S(1)}, bf16[4,16,1664]{2,1,0:T(8,128)(2,1)S(1)}, u32[]{:S(2)}, u32[]{:S(2)}) collective-permute-start(bf16[4,16,1664]{2,1,0:T(8,128)(2,1)S(1)} %collective-permute-done.4.refs_7_), channel_id=1, source_target_pairs={{0,2},{1,3},{2,0},{3,1},{4,6},{5,7},{6,4},{7,5},{8,10},{9,11},{10,... | collective-permute-start | bytes 638984 | tf_op jit(solution)/shard_map/ppermute | solution.py:836
  36.9 4.4 %collective-permute-start.9 = (bf16[4,16,1664]{2,1,0:T(8,128)(2,1)S(1)}, bf16[4,16,1664]{2,1,0:T(8,128)(2,1)S(1)}, u32[]{:S(2)}, u32[]{:S(2)}) collective-permute-start(bf16[4,16,1664]{2,1,0:T(8,128)(2,1)S(1)} %collective-permute-done.3.refs_6_), channel_id=1, source_target_pairs={{0,2},{1,3},{2,0},{3,1},{4,6},{5,7},{6,4},{7,5},{8,10},{9,11},{10,... | collective-permute-start | bytes 638984 | tf_op jit(solution)/shard_map/ppermute | solution.py:836
  37.8 15.3 %collective-permute-start.14 = (bf16[4,16,2560]{2,1,0:T(8,128)(2,1)S(1)}, bf16[4,16,2560]{2,1,0:T(8,128)(2,1)S(1)}, u32[]{:S(2)}, u32[]{:S(2)}) collective-permute-start(bf16[4,16,2560]{2,1,0:T(8,128)(2,1)S(1)} %bitcast.37), channel_id=1, source_target_pairs={{0,5},{1,4},{2,7},{3,6},{4,1},{5,0},{6,3},{7,2},{8,13},{9,12},{10,... | collective-permute-start | bytes 983048 | tf_op jit(solution)/shard_map/ppermute | solution.py:836
  40.3 17.0 %collective-permute-start.13 = (bf16[4,16,2560]{2,1,0:T(8,128)(2,1)S(1)}, bf16[4,16,2560]{2,1,0:T(8,128)(2,1)S(1)}, u32[]{:S(2)}, u32[]{:S(2)}) collective-permute-start(bf16[4,16,2560]{2,1,0:T(8,128)(2,1)S(1)} %bitcast.38), channel_id=1, source_target_pairs={{0,4},{1,5},{2,6},{3,7},{4,0},{5,1},{6,2},{7,3},{8,12},{9,13},{10,... | collective-permute-start | bytes 983048 | tf_op jit(solution)/shard_map/ppermute | solution.py:836
  40.7 18.5 %collective-permute-start.12 = (bf16[4,16,2560]{2,1,0:T(8,128)(2,1)S(1)}, bf16[4,16,2560]{2,1,0:T(8,128)(2,1)S(1)}, u32[]{:S(2)}, u32[]{:S(2)}) collective-permute-start(bf16[4,16,2560]{2,1,0:T(8,128)(2,1)S(1)} %bitcast.39), channel_id=1, source_target_pairs={{0,1},{1,0},{2,3},{3,2},{4,5},{5,4},{6,7},{7,6},{8,9},{9,8},{10,11... | collective-permute-start | bytes 983048 | tf_op jit(solution)/shard_map/ppermute | solution.py:836
  51.7 8.1 %collective-permute-start.15 = (bf16[4,16,2560]{2,1,0:T(8,128)(2,1)S(1)}, bf16[4,16,2560]{2,1,0:T(8,128)(2,1)S(1)}, u32[]{:S(2)}, u32[]{:S(2)}) collective-permute-start(bf16[4,16,2560]{2,1,0:T(8,128)(2,1)S(1)} %bitcast.40), channel_id=1, source_target_pairs={{0,2},{1,3},{2,0},{3,1},{4,6},{5,7},{6,4},{7,5},{8,10},{9,11},{10,... | collective-permute-start | bytes 983048 | tf_op jit(solution)/shard_map/ppermute | solution.py:836
  59.2 1.6 collective-permute-start.16
  59.2 2.1 collective-permute-start.17
  59.8 2.1 collective-permute-start.18
  130.1 58.1 %reduce-scatter.10.cloned.1.call-start = ((), (), s32[]{:S(2)}) async-start(), calls=%async_computation.7 | async-start | bytes 2621440
  154.5 72.9 %reduce-scatter.8.cloned.1.call-start = ((), (), s32[]{:S(2)}) async-start(), calls=%async_computation.5 | async-start | bytes 655360 | tf_op jit(solution)/shard_map/reduce_scatter | solution.py:908
  154.6 23.9 %collective-permute-start.20 = (bf16[16,16,2560]{2,1,0:T(8,128)(2,1)}, bf16[16,16,2560]{2,1,0:T(8,128)(2,1)S(1)}, u32[]{:S(2)}, u32[]{:S(2)}) collective-permute-start(bf16[16,16,2560]{2,1,0:T(8,128)(2,1)} %get-tuple-element.132), channel_id=1, source_target_pairs={{0,2},{1,3},{2,0},{3,1},{4,6},{5,7},{6,4},{7,5},{8,10},{9,11},{10,... | collective-permute-start | bytes 3932168 | tf_op jit(solution)/shard_map/ppermute | solution.py:836
  154.9 21.3 %copy-start.3 = (f32[3,16,128]{2,1,0:T(8,128)S(1)}, f32[3,16,128]{2,1,0:T(8,128)}, u32[]{:S(2)}) copy-start(f32[3,16,128]{2,1,0:T(8,128)} %get-tuple-element.163) | copy-start | bytes 73732
  154.9 21.3 %copy-start.4 = (f32[3,16,128]{2,1,0:T(8,128)S(1)}, f32[3,16,128]{2,1,0:T(8,128)}, u32[]{:S(2)}) copy-start(f32[3,16,128]{2,1,0:T(8,128)} %get-tuple-element.162) | copy-start | bytes 73732
  175.8 2.7 %collective-permute-start.19 = (bf16[16,16,1664]{2,1,0:T(8,128)(2,1)}, bf16[16,16,1664]{2,1,0:T(8,128)(2,1)S(1)}, u32[]{:S(2)}, u32[]{:S(2)}) collective-permute-start(bf16[16,16,1664]{2,1,0:T(8,128)(2,1)} %get-tuple-element.130), channel_id=1, source_target_pairs={{0,2},{1,3},{2,0},{3,1},{4,6},{5,7},{6,4},{7,5},{8,10},{9,11},{10,... | collective-permute-start | bytes 2555912 | tf_op jit(solution)/shard_map/ppermute | solution.py:836
  182.1 6.1 %copy-start.6 = (f32[3,4,8,128]{3,2,1,0:T(8,128)S(1)}, f32[3,4,8,128]{3,2,1,0:T(8,128)}, u32[]{:S(2)}) copy-start(f32[3,4,8,128]{3,2,1,0:T(8,128)} %get-tuple-element.164) | copy-start | bytes 147460
  188.4 15.4 %collective-permute-start.21 = (bf16[4,16,4224]{2,1,0:T(8,128)(2,1)}, bf16[4,16,4224]{2,1,0:T(8,128)(2,1)S(1)}, u32[]{:S(2)}, u32[]{:S(2)}) collective-permute-start(bf16[4,16,4224]{2,1,0:T(8,128)(2,1)} %get-tuple-element.136), channel_id=1, source_target_pairs={{0,1},{1,0},{2,3},{3,2},{4,5},{5,4},{6,7},{7,6},{8,9},{9,8},{10,11... | collective-permute-start | bytes 1622024 | tf_op jit(solution)/shard_map/ppermute | solution.py:836
  189.8 25.5 %collective-permute-start.22 = (bf16[4,16,4224]{2,1,0:T(8,128)(2,1)}, bf16[4,16,4224]{2,1,0:T(8,128)(2,1)S(1)}, u32[]{:S(2)}, u32[]{:S(2)}) collective-permute-start(bf16[4,16,4224]{2,1,0:T(8,128)(2,1)} %get-tuple-element.137), channel_id=1, source_target_pairs={{0,4},{1,5},{2,6},{3,7},{4,0},{5,1},{6,2},{7,3},{8,12},{9,13},{10,... | collective-permute-start | bytes 1622024 | tf_op jit(solution)/shard_map/ppermute | solution.py:836
  190.4 24.9 %collective-permute-start.23 = (bf16[4,16,4224]{2,1,0:T(8,128)(2,1)S(1)}, bf16[4,16,4224]{2,1,0:T(8,128)(2,1)S(1)}, u32[]{:S(2)}, u32[]{:S(2)}) collective-permute-start(bf16[4,16,4224]{2,1,0:T(8,128)(2,1)S(1)} %get-tuple-element.138), channel_id=1, source_target_pairs={{0,5},{1,4},{2,7},{3,6},{4,1},{5,0},{6,3},{7,2},{8,13},{9,12},{10,... | collective-permute-start | bytes 1622024 | tf_op jit(solution)/shard_map/ppermute | solution.py:836
  191.9 1.0 copy-start
  201.8 19.1 %copy-start.5 = (s32[12,256]{1,0:T(8,128)S(1)}, s32[12,256]{1,0:T(8,128)}, u32[]{:S(2)}) copy-start(s32[12,256]{1,0:T(8,128)} %refs_2_.7) | copy-start | bytes 36868
  216.5 12.8 %collective-permute-start.24 = (bf16[16,4224]{1,0:T(8,128)(2,1)S(1)}, bf16[16,4224]{1,0:T(8,128)(2,1)S(1)}, u32[]{:S(2)}, u32[]{:S(2)}) collective-permute-start(bf16[16,4224]{1,0:T(8,128)(2,1)S(1)} %get-tuple-element.141), channel_id=1, source_target_pairs={{0,8},{1,9},{2,10},{3,11},{4,12},{5,13},{6,14},{7,15},{8,0},{9,1},... | collective-permute-start | bytes 405512 | tf_op jit(solution)/shard_map/ppermute | solution.py:836
  218.0 12.1 %collective-permute-start.25 = (bf16[16,4224]{1,0:T(8,128)(2,1)S(1)}, bf16[16,4224]{1,0:T(8,128)(2,1)S(1)}, u32[]{:S(2)}, u32[]{:S(2)}) collective-permute-start(bf16[16,4224]{1,0:T(8,128)(2,1)S(1)} %get-tuple-element.142), channel_id=1, source_target_pairs={{0,16},{1,17},{2,18},{3,19},{4,20},{5,21},{6,22},{7,23},{8,24},{9,... | collective-permute-start | bytes 405512 | tf_op jit(solution)/shard_map/ppermute | solution.py:836
  220.4 9.6 %collective-permute-start.26 = (bf16[16,4224]{1,0:T(8,128)(2,1)S(1)}, bf16[16,4224]{1,0:T(8,128)(2,1)S(1)}, u32[]{:S(2)}, u32[]{:S(2)}) collective-permute-start(bf16[16,4224]{1,0:T(8,128)(2,1)S(1)} %get-tuple-element.143), channel_id=1, source_target_pairs={{0,24},{1,25},{2,26},{3,27},{4,28},{5,29},{6,30},{7,31},{8,16},{9,... | collective-permute-start | bytes 405512 | tf_op jit(solution)/shard_map/ppermute | solution.py:836
  221.0 10.7 %copy-start.7 = (f32[3,8,128]{2,1,0:T(8,128)S(1)}, f32[3,8,128]{2,1,0:T(8,128)}, u32[]{:S(2)}) copy-start(f32[3,8,128]{2,1,0:T(8,128)} %get-tuple-element.160) | copy-start | bytes 36868
  221.0 10.7 %copy-start.2 = (s32[12,128]{1,0:T(8,128)S(1)}, s32[12,128]{1,0:T(8,128)}, u32[]{:S(2)}) copy-start(s32[12,128]{1,0:T(8,128)} %refs_4_.7) | copy-start | bytes 18436
  227.4 0.9 copy-start.1
  232.6 11.4 %all-to-all-start = ((f32[32,1,128]{2,1,0:T(1,128)}), f32[32,1,128]{2,1,0:T(1,128)S(1)}, u32[]{:S(2)}, u32[]{:S(2)}) async-start(f32[32,1,128]{2,1,0:T(1,128)} %bitcast.28), calls=%async_computation.2 | async-start | bytes 32768 | tf_op jit(solution)/shard_map/all_to_all | solution.py:944
Sparse Core Ops, SparseCore 0:
  11.6 70.9 all-gather.2
  130.2 10.6 reduce-scatter.5
  154.7 33.4 reduce-scatter.9
  190.3 21.6 reduce-scatter.7
